TPU v7x, 128 devices: a whole 4x4x4 slice. The times are simulated.
128 devices in a mesh: lon: 16 (over x, z), lat: 8 (over y, core).
Axes of the slice: x: 4, y: 4, z: 4, core: 2. Of those that a mesh axis runs over, the one named last changes fastest.
Arguments:
- winds: float32 [2, 12, 256, 2048], P(None, None, 'lat', 'lon'), may hold values from -6 to 6
- coriolis: float32 [256], P('lat'), may hold values from 0.1 to 0.5
- rays: float32 [16, 8, 128, 4, 128], P('lon', 'lat'), as said below
- ray_cell: int32 [16, 8, 128, 128], P('lon', 'lat'), may hold values from 0 to 4095
- ray_level: int32 [16, 8, 128, 128], P('lon', 'lat'), may hold values from 0 to 11
- turning: int32 [16, 8, 128, 128], P('lon', 'lat'), may hold values 0 or 1
- leaving: int32 [16, 8, 8, 8], P('lon', 'lat'), may hold values from 0 to 127, as said below
- leave_count: int32 [16, 8, 8], P('lon', 'lat'), may hold values from 0 to 8, as said below
Outputs:
- rays_out: float32 [16, 8, 128, 4, 128], P('lon', 'lat')
- arrived: float32 [16, 8, 8, 8, 4, 128], P('lon', 'lat')
- tendency: float32 [2, 12, 256, 2048], P(None, None, 'lat', 'lon')
Inputs may be any that keep to these rules, and one draw needn't show every extreme that they name: `rays`: the fourth ray field, the wave action, is positive. `leaving`: the block numbers in one tile's lists are distinct. `leave_count`: lists pointing beyond the latitude ends have count zero.
All inputs are finite; a program needn't handle non-finite values. No bound on the sum of `turning` on one device may be relied on, other than what follows from the above.
Results may differ from a plain program's by a relative error of at most 0.000078.
Values sent between devices are 32-bit elements; how exact they have to be, the bound alone decides.
A program may use at most 128 MiB of HBM per device.

v0:
```python
import jax
import jax.numpy as jnp
from jax import lax
from jax.sharding import PartitionSpec as P

STEP = 0.1
DIRS = ((0, 1), (0, -1), (1, 0), (-1, 0), (1, 1), (1, -1), (-1, 1), (-1, -1))
HIGH = lax.Precision.HIGHEST


def padded_2(shard, sides, width, wrap):
    for axis, dim in sides:
        peers, length = (lax.axis_size(axis), shard.shape[dim])
        up = [(i, (i + 1) % peers) for i in range(peers if wrap else peers - 1)]
        down = [(j, i) for i, j in up]
        last = lax.slice_in_dim(shard, length - width, length, axis=dim)
        first = lax.slice_in_dim(shard, 0, width, axis=dim)
        before = lax.ppermute(last, axis, up)
        after = lax.ppermute(first, axis, down)
        shard = jnp.concatenate([before, shard, after], axis=dim)
    return shard


def passed_along(shard, axis, by):
    peers = lax.axis_size(axis)
    return lax.ppermute(shard, axis, [(i, (i + by) % peers) for i in range(peers)])


def passed_along_2(block, axis, distance):
    devices = range(lax.axis_size(axis))
    route = [(i - distance, i) for i in devices if i - distance in devices]
    return lax.ppermute(block, axis, route)


def diff_open(field, axis):
    widths = [(1, 1) if a == axis else (0, 0) for a in range(field.ndim)]
    padded = jnp.pad(field, widths)
    count = field.shape[axis]
    upper = lax.slice_in_dim(padded, 2, count + 2, axis=axis)
    lower = lax.slice_in_dim(padded, 0, count, axis=axis)
    return (upper - lower) * 0.5


def propagate(wave_k, wave_l, wave_m, action, sample, fcor, turn):
    new_k = wave_k - STEP * (wave_k * sample[0] + wave_l * sample[1])
    new_l = wave_l - STEP * (wave_k * sample[2] + wave_l * sample[3])
    new_m = wave_m - STEP * (wave_k * sample[4] + wave_l * sample[5])
    new_m = jnp.where(turn == 1, -new_m, new_m)
    horiz = new_k * new_k + new_l * new_l
    total = horiz + new_m * new_m + 1.0
    fsq = fcor * fcor
    freq2 = (horiz + fsq * (new_m * new_m + 1.0)) / total
    freq = jnp.sqrt(freq2)
    group_x = new_k * (1.0 - freq2) / (freq * total)
    group_z = new_m * (fsq - freq2) / (freq * total)
    return (
        new_k,
        new_l,
        new_m,
        group_z * new_k * action,
        group_z * new_l * action,
        group_x * new_k * action,
    )


def on_device(winds, coriolis, rays, ray_cell, ray_level, turning, leaving, leave_count):
    levels = winds.shape[1]
    rows_y = winds.shape[2]
    cells_x = winds.shape[3]
    ncell = rows_y * cells_x
    wide_x = padded_2(winds, (("lon", 3),), 1, True)
    wide_y = padded_2(winds, (("lat", 2),), 1, False)
    grad = jnp.concatenate(
        [
            (wide_x[..., 2:] - wide_x[..., :-2]) * 0.5,
            (wide_y[:, :, 2:] - wide_y[:, :, :-2]) * 0.5,
            diff_open(winds, 1),
        ],
        axis=0,
    )
    grad_flat = grad.reshape(6, levels * ncell)
    ray_data = rays[0, 0]
    cell_data = ray_cell[0, 0]
    level_data = ray_level[0, 0]
    turn_data = turning[0, 0]
    nblocks = ray_data.shape[0]
    width = ray_data.shape[2]
    group = 8
    cell_ids = jnp.arange(ncell, dtype=jnp.int32)
    level_ids = jnp.arange(levels, dtype=jnp.int32)

    def one_group(carry, index):
        start = index * group
        part = lax.dynamic_slice_in_dim(ray_data, start, group, 0)
        cells = lax.dynamic_slice_in_dim(cell_data, start, group, 0).reshape(-1)
        lvls = lax.dynamic_slice_in_dim(level_data, start, group, 0).reshape(-1)
        turn = lax.dynamic_slice_in_dim(turn_data, start, group, 0).reshape(-1)
        fields = jnp.transpose(part, (1, 0, 2)).reshape(4, -1)
        sample = jnp.take(grad_flat, lvls * ncell + cells, axis=1)
        fcor = jnp.take(coriolis, cells // cells_x, axis=0)
        new_k, new_l, new_m, flux_a, flux_b, flux_c = propagate(
            fields[0], fields[1], fields[2], fields[3], sample, fcor, turn
        )
        onehot = (cells[:, None] == cell_ids[None, :]).astype(jnp.float32)
        level_hot = (lvls[None, :] == level_ids[:, None]).astype(jnp.float32)
        weights = (jnp.stack([flux_a, flux_b, flux_c])[:, None, :] * level_hot[None]).reshape(
            3 * levels, -1
        )
        carry = carry + jnp.dot(weights, onehot, precision=HIGH)
        updated = jnp.stack([new_k, new_l, new_m, fields[3]]).reshape(4, group, width)
        return (carry, jnp.transpose(updated, (1, 0, 2)))

    deposit, pieces = lax.scan(
        one_group,
        jnp.zeros((3 * levels, ncell), jnp.float32),
        jnp.arange(nblocks // group, dtype=jnp.int32),
    )
    rays_new = pieces.reshape(nblocks, 4, width)
    deposit = deposit.reshape(3, levels, rows_y, cells_x)
    leave_ids = leaving[0, 0]
    counts = leave_count[0, 0]
    slots = leave_ids.shape[1]
    chosen = rays_new[leave_ids]
    live = jnp.arange(slots, dtype=jnp.int32)[None, :] < counts[:, None]
    outgoing = jnp.where(live[:, :, None, None], chosen, jnp.float32(0.0))
    gathered = []
    for which in range(8):
        dlat, dlon = DIRS[which]
        piece = outgoing[which]
        if dlon != 0:
            piece = passed_along(piece, "lon", dlon)
        if dlat != 0:
            piece = passed_along_2(piece, "lat", dlat)
        gathered.append(piece)
    arrived = jnp.stack(gathered)
    zonal = padded_2(deposit[2], (("lon", 2),), 1, True)
    east = -diff_open(deposit[0], 0) - (zonal[..., 2:] - zonal[..., :-2]) * 0.5
    north = -diff_open(deposit[1], 0)
    tendency = jnp.stack([east, north])
    return (rays_new[None, None], arrived[None, None], tendency)


def solution(mesh):
    placed = (
        P(None, None, "lat", "lon"),
        P("lat"),
        P("lon", "lat", None, None, None),
        P("lon", "lat", None, None),
        P("lon", "lat", None, None),
        P("lon", "lat", None, None),
        P("lon", "lat", None, None),
        P("lon", "lat", None),
    )
    return jax.shard_map(
        on_device,
        mesh=mesh,
        in_specs=placed,
        out_specs=(
            P("lon", "lat", None, None, None),
            P("lon", "lat", None, None, None, None),
            P(None, None, "lat", "lon"),
        ),
        check_vma=False,
    )
```

profile of v0, /device:TPU:1, one launch (start us, length us, event | category | flops | bytes accessed | tf_op | source)
XLA Modules:
  0.0 768.8 jit_solution(12392037807676030385)
XLA Ops:
  1.9 6.8 collective-permute-start
  24.3 12.8 %copy.91 = f32[6,12,32,128]{0,3,2,1:T(8,128)} copy(f32[6,12,32,128]{3,2,1,0:T(8,128)S(1)} %pad_maximum_fusion.1) | data formatting | bytes 2359296 | tf_op jit(solution)/shard_map/concatenate | solution.py:73
  37.1 686.5 %while.15 = (s32[]{:T(128)}, f32[36,4096]{1,0:T(8,128)S(1)}, f32[16,8,4,128]{3,1,2,0:T(8,128)S(1)}, s32[16]{0:T(128)S(1)}, s32[128,128]{1,0:T(8,128)}, /*index=5...) while((s32[]{:T(128)}, f32[36,4096]{1,0:T(8,128)S(1)}, ...), condition=%wide.region_1.2_spmd.clone, body=%wide.region_0.1_spmd.clone.sunk | while | flops 1816683520 | bytes 2398813 | solution.py:113
  39.8 4.4 compare_select_fusion.21
  45.2 15.4 %select_select_fusion.2 = f32[1024]{0:T(1024)S(1)} fusion(pred[1024]{0:T(1024)(128)(4,1)S(1)} %get-tuple-element.457, pred[1024]{0:T(1024)(128)(4,1)S(1)} %get-tuple-element.458, pred[1024]{0:T(1024)(128)(4,1)S(1)} %get-tuple-element.459, pred[1024]{0:T(1024)(128)(4,1)S(1)} %get-tuple-element.460, pred[1024]{0:T(1024)(128)(4,1)S(1)} %get-tuple-element.461, ...), kind=kLoop, calls=%fused_computation.71.clone.1 | loop fusion | flops 25600 | bytes 33892 | tf_op jit(solution)/shard_map/while/body/eval_jaxpr/jit(_take)/gather | solution.py:100
  61.4 11.0 %gather_fusion = f32[1024,6]{1,0:T(8,128)S(1)} fusion(f32[6,49152]{0,1:T(8,128)} %get-tuple-element.552, s32[1024]{0:T(1024)S(1)} %broadcast_clamp_fusion.2), kind=kCustom, calls=%fused_computation.clone.clone.1 | custom fusion | bytes 53248 | tf_op jit(solution)/shard_map/while/body/eval_jaxpr/jit(_take)/gather | solution.py:99
  73.5 6.5 fusion.53
  82.7 4.4 compare_select_fusion.21
  88.1 15.4 %select_select_fusion.2 = f32[1024]{0:T(1024)S(1)} fusion(pred[1024]{0:T(1024)(128)(4,1)S(1)} %get-tuple-element.457, pred[1024]{0:T(1024)(128)(4,1)S(1)} %get-tuple-element.458, pred[1024]{0:T(1024)(128)(4,1)S(1)} %get-tuple-element.459, pred[1024]{0:T(1024)(128)(4,1)S(1)} %get-tuple-element.460, pred[1024]{0:T(1024)(128)(4,1)S(1)} %get-tuple-element.461, ...), kind=kLoop, calls=%fused_computation.71.clone.1 | loop fusion | flops 25600 | bytes 33892 | tf_op jit(solution)/shard_map/while/body/eval_jaxpr/jit(_take)/gather | solution.py:100
  104.3 11.0 %gather_fusion = f32[1024,6]{1,0:T(8,128)S(1)} fusion(f32[6,49152]{0,1:T(8,128)} %get-tuple-element.552, s32[1024]{0:T(1024)S(1)} %broadcast_clamp_fusion.2), kind=kCustom, calls=%fused_computation.clone.clone.1 | custom fusion | bytes 53248 | tf_op jit(solution)/shard_map/while/body/eval_jaxpr/jit(_take)/gather | solution.py:99
  116.5 6.5 fusion.53
  125.6 4.4 compare_select_fusion.21
  131.0 15.4 %select_select_fusion.2 = f32[1024]{0:T(1024)S(1)} fusion(pred[1024]{0:T(1024)(128)(4,1)S(1)} %get-tuple-element.457, pred[1024]{0:T(1024)(128)(4,1)S(1)} %get-tuple-element.458, pred[1024]{0:T(1024)(128)(4,1)S(1)} %get-tuple-element.459, pred[1024]{0:T(1024)(128)(4,1)S(1)} %get-tuple-element.460, pred[1024]{0:T(1024)(128)(4,1)S(1)} %get-tuple-element.461, ...), kind=kLoop, calls=%fused_computation.71.clone.1 | loop fusion | flops 25600 | bytes 33892 | tf_op jit(solution)/shard_map/while/body/eval_jaxpr/jit(_take)/gather | solution.py:100
  147.2 11.0 %gather_fusion = f32[1024,6]{1,0:T(8,128)S(1)} fusion(f32[6,49152]{0,1:T(8,128)} %get-tuple-element.552, s32[1024]{0:T(1024)S(1)} %broadcast_clamp_fusion.2), kind=kCustom, calls=%fused_computation.clone.clone.1 | custom fusion | bytes 53248 | tf_op jit(solution)/shard_map/while/body/eval_jaxpr/jit(_take)/gather | solution.py:99
  159.4 6.5 fusion.53
  168.5 4.4 compare_select_fusion.21
  173.9 15.4 %select_select_fusion.2 = f32[1024]{0:T(1024)S(1)} fusion(pred[1024]{0:T(1024)(128)(4,1)S(1)} %get-tuple-element.457, pred[1024]{0:T(1024)(128)(4,1)S(1)} %get-tuple-element.458, pred[1024]{0:T(1024)(128)(4,1)S(1)} %get-tuple-element.459, pred[1024]{0:T(1024)(128)(4,1)S(1)} %get-tuple-element.460, pred[1024]{0:T(1024)(128)(4,1)S(1)} %get-tuple-element.461, ...), kind=kLoop, calls=%fused_computation.71.clone.1 | loop fusion | flops 25600 | bytes 33892 | tf_op jit(solution)/shard_map/while/body/eval_jaxpr/jit(_take)/gather | solution.py:100
  190.1 11.0 %gather_fusion = f32[1024,6]{1,0:T(8,128)S(1)} fusion(f32[6,49152]{0,1:T(8,128)} %get-tuple-element.552, s32[1024]{0:T(1024)S(1)} %broadcast_clamp_fusion.2), kind=kCustom, calls=%fused_computation.clone.clone.1 | custom fusion | bytes 53248 | tf_op jit(solution)/shard_map/while/body/eval_jaxpr/jit(_take)/gather | solution.py:99
  202.3 6.5 fusion.53
  211.4 4.4 compare_select_fusion.21
  216.9 15.4 %select_select_fusion.2 = f32[1024]{0:T(1024)S(1)} fusion(pred[1024]{0:T(1024)(128)(4,1)S(1)} %get-tuple-element.457, pred[1024]{0:T(1024)(128)(4,1)S(1)} %get-tuple-element.458, pred[1024]{0:T(1024)(128)(4,1)S(1)} %get-tuple-element.459, pred[1024]{0:T(1024)(128)(4,1)S(1)} %get-tuple-element.460, pred[1024]{0:T(1024)(128)(4,1)S(1)} %get-tuple-element.461, ...), kind=kLoop, calls=%fused_computation.71.clone.1 | loop fusion | flops 25600 | bytes 33892 | tf_op jit(solution)/shard_map/while/body/eval_jaxpr/jit(_take)/gather | solution.py:100
  233.0 11.0 %gather_fusion = f32[1024,6]{1,0:T(8,128)S(1)} fusion(f32[6,49152]{0,1:T(8,128)} %get-tuple-element.552, s32[1024]{0:T(1024)S(1)} %broadcast_clamp_fusion.2), kind=kCustom, calls=%fused_computation.clone.clone.1 | custom fusion | bytes 53248 | tf_op jit(solution)/shard_map/while/body/eval_jaxpr/jit(_take)/gather | solution.py:99
  245.2 6.5 fusion.53
  254.3 4.4 compare_select_fusion.21
  259.8 15.4 %select_select_fusion.2 = f32[1024]{0:T(1024)S(1)} fusion(pred[1024]{0:T(1024)(128)(4,1)S(1)} %get-tuple-element.457, pred[1024]{0:T(1024)(128)(4,1)S(1)} %get-tuple-element.458, pred[1024]{0:T(1024)(128)(4,1)S(1)} %get-tuple-element.459, pred[1024]{0:T(1024)(128)(4,1)S(1)} %get-tuple-element.460, pred[1024]{0:T(1024)(128)(4,1)S(1)} %get-tuple-element.461, ...), kind=kLoop, calls=%fused_computation.71.clone.1 | loop fusion | flops 25600 | bytes 33892 | tf_op jit(solution)/shard_map/while/body/eval_jaxpr/jit(_take)/gather | solution.py:100
  275.9 11.0 %gather_fusion = f32[1024,6]{1,0:T(8,128)S(1)} fusion(f32[6,49152]{0,1:T(8,128)} %get-tuple-element.552, s32[1024]{0:T(1024)S(1)} %broadcast_clamp_fusion.2), kind=kCustom, calls=%fused_computation.clone.clone.1 | custom fusion | bytes 53248 | tf_op jit(solution)/shard_map/while/body/eval_jaxpr/jit(_take)/gather | solution.py:99
  288.1 6.5 fusion.53
  302.7 15.4 %select_select_fusion.2 = f32[1024]{0:T(1024)S(1)} fusion(pred[1024]{0:T(1024)(128)(4,1)S(1)} %get-tuple-element.457, pred[1024]{0:T(1024)(128)(4,1)S(1)} %get-tuple-element.458, pred[1024]{0:T(1024)(128)(4,1)S(1)} %get-tuple-element.459, pred[1024]{0:T(1024)(128)(4,1)S(1)} %get-tuple-element.460, pred[1024]{0:T(1024)(128)(4,1)S(1)} %get-tuple-element.461, ...), kind=kLoop, calls=%fused_computation.71.clone.1 | loop fusion | flops 25600 | bytes 33892 | tf_op jit(solution)/shard_map/while/body/eval_jaxpr/jit(_take)/gather | solution.py:100
  318.8 11.0 %gather_fusion = f32[1024,6]{1,0:T(8,128)S(1)} fusion(f32[6,49152]{0,1:T(8,128)} %get-tuple-element.552, s32[1024]{0:T(1024)S(1)} %broadcast_clamp_fusion.2), kind=kCustom, calls=%fused_computation.clone.clone.1 | custom fusion | bytes 53248 | tf_op jit(solution)/shard_map/while/body/eval_jaxpr/jit(_take)/gather | solution.py:99
  331.0 6.5 fusion.53
  345.6 15.4 %select_select_fusion.2 = f32[1024]{0:T(1024)S(1)} fusion(pred[1024]{0:T(1024)(128)(4,1)S(1)} %get-tuple-element.457, pred[1024]{0:T(1024)(128)(4,1)S(1)} %get-tuple-element.458, pred[1024]{0:T(1024)(128)(4,1)S(1)} %get-tuple-element.459, pred[1024]{0:T(1024)(128)(4,1)S(1)} %get-tuple-element.460, pred[1024]{0:T(1024)(128)(4,1)S(1)} %get-tuple-element.461, ...), kind=kLoop, calls=%fused_computation.71.clone.1 | loop fusion | flops 25600 | bytes 33892 | tf_op jit(solution)/shard_map/while/body/eval_jaxpr/jit(_take)/gather | solution.py:100
  361.7 11.0 %gather_fusion = f32[1024,6]{1,0:T(8,128)S(1)} fusion(f32[6,49152]{0,1:T(8,128)} %get-tuple-element.552, s32[1024]{0:T(1024)S(1)} %broadcast_clamp_fusion.2), kind=kCustom, calls=%fused_computation.clone.clone.1 | custom fusion | bytes 53248 | tf_op jit(solution)/shard_map/while/body/eval_jaxpr/jit(_take)/gather | solution.py:99
  373.9 6.5 fusion.53
  383.0 4.4 compare_select_fusion.21
  388.5 15.4 %select_select_fusion.2 = f32[1024]{0:T(1024)S(1)} fusion(pred[1024]{0:T(1024)(128)(4,1)S(1)} %get-tuple-element.457, pred[1024]{0:T(1024)(128)(4,1)S(1)} %get-tuple-element.458, pred[1024]{0:T(1024)(128)(4,1)S(1)} %get-tuple-element.459, pred[1024]{0:T(1024)(128)(4,1)S(1)} %get-tuple-element.460, pred[1024]{0:T(1024)(128)(4,1)S(1)} %get-tuple-element.461, ...), kind=kLoop, calls=%fused_computation.71.clone.1 | loop fusion | flops 25600 | bytes 33892 | tf_op jit(solution)/shard_map/while/body/eval_jaxpr/jit(_take)/gather | solution.py:100
  404.6 11.0 %gather_fusion = f32[1024,6]{1,0:T(8,128)S(1)} fusion(f32[6,49152]{0,1:T(8,128)} %get-tuple-element.552, s32[1024]{0:T(1024)S(1)} %broadcast_clamp_fusion.2), kind=kCustom, calls=%fused_computation.clone.clone.1 | custom fusion | bytes 53248 | tf_op jit(solution)/shard_map/while/body/eval_jaxpr/jit(_take)/gather | solution.py:99
  416.8 6.5 fusion.53
  425.9 4.4 compare_select_fusion.21
  431.4 15.4 %select_select_fusion.2 = f32[1024]{0:T(1024)S(1)} fusion(pred[1024]{0:T(1024)(128)(4,1)S(1)} %get-tuple-element.457, pred[1024]{0:T(1024)(128)(4,1)S(1)} %get-tuple-element.458, pred[1024]{0:T(1024)(128)(4,1)S(1)} %get-tuple-element.459, pred[1024]{0:T(1024)(128)(4,1)S(1)} %get-tuple-element.460, pred[1024]{0:T(1024)(128)(4,1)S(1)} %get-tuple-element.461, ...), kind=kLoop, calls=%fused_computation.71.clone.1 | loop fusion | flops 25600 | bytes 33892 | tf_op jit(solution)/shard_map/while/body/eval_jaxpr/jit(_take)/gather | solution.py:100
  447.5 11.0 %gather_fusion = f32[1024,6]{1,0:T(8,128)S(1)} fusion(f32[6,49152]{0,1:T(8,128)} %get-tuple-element.552, s32[1024]{0:T(1024)S(1)} %broadcast_clamp_fusion.2), kind=kCustom, calls=%fused_computation.clone.clone.1 | custom fusion | bytes 53248 | tf_op jit(solution)/shard_map/while/body/eval_jaxpr/jit(_take)/gather | solution.py:99
  459.7 6.5 fusion.53
  468.8 4.4 compare_select_fusion.21
  474.3 15.4 %select_select_fusion.2 = f32[1024]{0:T(1024)S(1)} fusion(pred[1024]{0:T(1024)(128)(4,1)S(1)} %get-tuple-element.457, pred[1024]{0:T(1024)(128)(4,1)S(1)} %get-tuple-element.458, pred[1024]{0:T(1024)(128)(4,1)S(1)} %get-tuple-element.459, pred[1024]{0:T(1024)(128)(4,1)S(1)} %get-tuple-element.460, pred[1024]{0:T(1024)(128)(4,1)S(1)} %get-tuple-element.461, ...), kind=kLoop, calls=%fused_computation.71.clone.1 | loop fusion | flops 25600 | bytes 33892 | tf_op jit(solution)/shard_map/while/body/eval_jaxpr/jit(_take)/gather | solution.py:100
  490.4 11.0 %gather_fusion = f32[1024,6]{1,0:T(8,128)S(1)} fusion(f32[6,49152]{0,1:T(8,128)} %get-tuple-element.552, s32[1024]{0:T(1024)S(1)} %broadcast_clamp_fusion.2), kind=kCustom, calls=%fused_computation.clone.clone.1 | custom fusion | bytes 53248 | tf_op jit(solution)/shard_map/while/body/eval_jaxpr/jit(_take)/gather | solution.py:99
  502.6 6.5 fusion.53
  517.2 15.4 %select_select_fusion.2 = f32[1024]{0:T(1024)S(1)} fusion(pred[1024]{0:T(1024)(128)(4,1)S(1)} %get-tuple-element.457, pred[1024]{0:T(1024)(128)(4,1)S(1)} %get-tuple-element.458, pred[1024]{0:T(1024)(128)(4,1)S(1)} %get-tuple-element.459, pred[1024]{0:T(1024)(128)(4,1)S(1)} %get-tuple-element.460, pred[1024]{0:T(1024)(128)(4,1)S(1)} %get-tuple-element.461, ...), kind=kLoop, calls=%fused_computation.71.clone.1 | loop fusion | flops 25600 | bytes 33892 | tf_op jit(solution)/shard_map/while/body/eval_jaxpr/jit(_take)/gather | solution.py:100
  533.3 11.0 %gather_fusion = f32[1024,6]{1,0:T(8,128)S(1)} fusion(f32[6,49152]{0,1:T(8,128)} %get-tuple-element.552, s32[1024]{0:T(1024)S(1)} %broadcast_clamp_fusion.2), kind=kCustom, calls=%fused_computation.clone.clone.1 | custom fusion | bytes 53248 | tf_op jit(solution)/shard_map/while/body/eval_jaxpr/jit(_take)/gather | solution.py:99
  545.5 6.5 fusion.53
  560.1 15.4 %select_select_fusion.2 = f32[1024]{0:T(1024)S(1)} fusion(pred[1024]{0:T(1024)(128)(4,1)S(1)} %get-tuple-element.457, pred[1024]{0:T(1024)(128)(4,1)S(1)} %get-tuple-element.458, pred[1024]{0:T(1024)(128)(4,1)S(1)} %get-tuple-element.459, pred[1024]{0:T(1024)(128)(4,1)S(1)} %get-tuple-element.460, pred[1024]{0:T(1024)(128)(4,1)S(1)} %get-tuple-element.461, ...), kind=kLoop, calls=%fused_computation.71.clone.1 | loop fusion | flops 25600 | bytes 33892 | tf_op jit(solution)/shard_map/while/body/eval_jaxpr/jit(_take)/gather | solution.py:100
  576.2 11.0 %gather_fusion = f32[1024,6]{1,0:T(8,128)S(1)} fusion(f32[6,49152]{0,1:T(8,128)} %get-tuple-element.552, s32[1024]{0:T(1024)S(1)} %broadcast_clamp_fusion.2), kind=kCustom, calls=%fused_computation.clone.clone.1 | custom fusion | bytes 53248 | tf_op jit(solution)/shard_map/while/body/eval_jaxpr/jit(_take)/gather | solution.py:99
  588.4 6.5 fusion.53
  603.0 15.4 %select_select_fusion.2 = f32[1024]{0:T(1024)S(1)} fusion(pred[1024]{0:T(1024)(128)(4,1)S(1)} %get-tuple-element.457, pred[1024]{0:T(1024)(128)(4,1)S(1)} %get-tuple-element.458, pred[1024]{0:T(1024)(128)(4,1)S(1)} %get-tuple-element.459, pred[1024]{0:T(1024)(128)(4,1)S(1)} %get-tuple-element.460, pred[1024]{0:T(1024)(128)(4,1)S(1)} %get-tuple-element.461, ...), kind=kLoop, calls=%fused_computation.71.clone.1 | loop fusion | flops 25600 | bytes 33892 | tf_op jit(solution)/shard_map/while/body/eval_jaxpr/jit(_take)/gather | solution.py:100
  619.2 11.0 %gather_fusion = f32[1024,6]{1,0:T(8,128)S(1)} fusion(f32[6,49152]{0,1:T(8,128)} %get-tuple-element.552, s32[1024]{0:T(1024)S(1)} %broadcast_clamp_fusion.2), kind=kCustom, calls=%fused_computation.clone.clone.1 | custom fusion | bytes 53248 | tf_op jit(solution)/shard_map/while/body/eval_jaxpr/jit(_take)/gather | solution.py:99
  631.3 6.5 fusion.53
  645.9 15.4 %select_select_fusion.2 = f32[1024]{0:T(1024)S(1)} fusion(pred[1024]{0:T(1024)(128)(4,1)S(1)} %get-tuple-element.457, pred[1024]{0:T(1024)(128)(4,1)S(1)} %get-tuple-element.458, pred[1024]{0:T(1024)(128)(4,1)S(1)} %get-tuple-element.459, pred[1024]{0:T(1024)(128)(4,1)S(1)} %get-tuple-element.460, pred[1024]{0:T(1024)(128)(4,1)S(1)} %get-tuple-element.461, ...), kind=kLoop, calls=%fused_computation.71.clone.1 | loop fusion | flops 25600 | bytes 33892 | tf_op jit(solution)/shard_map/while/body/eval_jaxpr/jit(_take)/gather | solution.py:100
  662.1 11.0 %gather_fusion = f32[1024,6]{1,0:T(8,128)S(1)} fusion(f32[6,49152]{0,1:T(8,128)} %get-tuple-element.552, s32[1024]{0:T(1024)S(1)} %broadcast_clamp_fusion.2), kind=kCustom, calls=%fused_computation.clone.clone.1 | custom fusion | bytes 53248 | tf_op jit(solution)/shard_map/while/body/eval_jaxpr/jit(_take)/gather | solution.py:99
  674.2 6.5 fusion.53
  688.8 15.4 %select_select_fusion.2 = f32[1024]{0:T(1024)S(1)} fusion(pred[1024]{0:T(1024)(128)(4,1)S(1)} %get-tuple-element.457, pred[1024]{0:T(1024)(128)(4,1)S(1)} %get-tuple-element.458, pred[1024]{0:T(1024)(128)(4,1)S(1)} %get-tuple-element.459, pred[1024]{0:T(1024)(128)(4,1)S(1)} %get-tuple-element.460, pred[1024]{0:T(1024)(128)(4,1)S(1)} %get-tuple-element.461, ...), kind=kLoop, calls=%fused_computation.71.clone.1 | loop fusion | flops 25600 | bytes 33892 | tf_op jit(solution)/shard_map/while/body/eval_jaxpr/jit(_take)/gather | solution.py:100
  705.0 11.0 %gather_fusion = f32[1024,6]{1,0:T(8,128)S(1)} fusion(f32[6,49152]{0,1:T(8,128)} %get-tuple-element.552, s32[1024]{0:T(1024)S(1)} %broadcast_clamp_fusion.2), kind=kCustom, calls=%fused_computation.clone.clone.1 | custom fusion | bytes 53248 | tf_op jit(solution)/shard_map/while/body/eval_jaxpr/jit(_take)/gather | solution.py:99
  717.1 6.5 fusion.53
  725.5 4.8 collective-permute-start.5
  730.3 5.5 collective-permute-start.6
  747.5 4.8 collective-permute-start.14
  754.3 4.5 collective-permute-start.9
  (399 shorter events, 150.7 us)
Async XLA Ops:
  1.9 16.3 %collective-permute-start = (f32[2,12,32,1]{3,2,1,0:T(8,128)S(1)}, f32[2,12,32,1]{3,2,1,0:T(8,128)S(1)}, u32[]{:S(2)}, u32[]{:S(2)}) collective-permute-start(f32[2,12,32,1]{3,2,1,0:T(8,128)S(1)} %get-tuple-element.293), channel_id=1, source_target_pairs={{8,0},{16,8},{24,16},{32,24},{40,32},{48,40},{56,48},{64,56},{72,6... | collective-permute-start | bytes 9224 | tf_op jit(solution)/shard_map/ppermute | solution.py:19
  8.8 13.0 %collective-permute-start.1 = (f32[2,12,32,1]{3,2,1,0:T(8,128)S(1)}, f32[2,12,32,1]{3,2,1,0:T(8,128)S(1)}, u32[]{:S(2)}, u32[]{:S(2)}) collective-permute-start(f32[2,12,32,1]{3,2,1,0:T(8,128)S(1)} %get-tuple-element.294), channel_id=1, source_target_pairs={{0,8},{8,16},{16,24},{24,32},{32,40},{40,48},{48,56},{56,64},{64,7... | collective-permute-start | bytes 9224 | tf_op jit(solution)/shard_map/ppermute | solution.py:18
  9.7 12.0 %collective-permute-start.2 = (f32[2,12,1,128]{3,2,1,0:T(1,128)S(1)}, f32[2,12,1,128]{3,2,1,0:T(1,128)S(1)}, u32[]{:S(2)}, u32[]{:S(2)}) collective-permute-start(f32[2,12,1,128]{3,2,1,0:T(1,128)S(1)} %get-tuple-element.295), channel_id=1, source_target_pairs={{1,0},{2,1},{3,2},{4,3},{5,4},{6,5},{7,6},{9,8},{10,9},{11,10},{12... | collective-permute-start | bytes 36872 | tf_op jit(solution)/shard_map/ppermute | solution.py:19
  12.6 9.2 %collective-permute-start.3 = (f32[2,12,1,128]{3,2,1,0:T(1,128)S(1)}, f32[2,12,1,128]{3,2,1,0:T(1,128)S(1)}, u32[]{:S(2)}, u32[]{:S(2)}) collective-permute-start(f32[2,12,1,128]{3,2,1,0:T(1,128)S(1)} %get-tuple-element.296), channel_id=1, source_target_pairs={{0,1},{1,2},{2,3},{3,4},{4,5},{5,6},{6,7},{8,9},{9,10},{10,11},{11... | collective-permute-start | bytes 36872 | tf_op jit(solution)/shard_map/ppermute | solution.py:18
  24.3 12.8 %copy-start = (f32[32]{0:T(128)S(1)}, f32[32]{0:T(128)}, u32[]{:S(2)}) copy-start(f32[32]{0:T(128)} %param.11) | copy-start | bytes 388
  725.4 22.0 %collective-permute-start.4 = (f32[8,4,128]{2,1,0:T(4,128)S(1)}, f32[8,4,128]{2,1,0:T(4,128)S(1)}, u32[]{:S(2)}, u32[]{:S(2)}) collective-permute-start(f32[8,4,128]{2,1,0:T(4,128)S(1)} %get-tuple-element.306), channel_id=1, source_target_pairs={{0,8},{8,16},{16,24},{24,32},{32,40},{40,48},{48,56},{56,64},{64,7... | collective-permute-start | bytes 49160 | tf_op jit(solution)/shard_map/ppermute | solution.py:26
  725.5 22.0 %collective-permute-start.5 = (f32[8,4,128]{2,1,0:T(4,128)S(1)}, f32[8,4,128]{2,1,0:T(4,128)S(1)}, u32[]{:S(2)}, u32[]{:S(2)}) collective-permute-start(f32[8,4,128]{2,1,0:T(4,128)S(1)} %get-tuple-element.305), channel_id=1, source_target_pairs={{0,120},{8,0},{16,8},{24,16},{32,24},{40,32},{48,40},{56,48},{64,5... | collective-permute-start | bytes 49160 | tf_op jit(solution)/shard_map/ppermute | solution.py:26
  730.3 22.0 %collective-permute-start.6 = (f32[8,4,128]{2,1,0:T(4,128)S(1)}, f32[8,4,128]{2,1,0:T(4,128)S(1)}, u32[]{:S(2)}, u32[]{:S(2)}) collective-permute-start(f32[8,4,128]{2,1,0:T(4,128)S(1)} %get-tuple-element.304), channel_id=1, source_target_pairs={{0,1},{1,2},{2,3},{3,4},{4,5},{5,6},{6,7},{8,9},{9,10},{10,11},{11... | collective-permute-start | bytes 49160 | tf_op jit(solution)/shard_map/ppermute | solution.py:32
  736.0 5.7 collective-permute-start.16
  736.1 8.7 %collective-permute-start.17 = (f32[12,32,1]{2,1,0:T(8,128)S(1)}, f32[12,32,1]{2,1,0:T(8,128)S(1)}, u32[]{:S(2)}, u32[]{:S(2)}) collective-permute-start(f32[12,32,1]{2,1,0:T(8,128)S(1)} %get-tuple-element.298), channel_id=1, source_target_pairs={{0,8},{8,16},{16,24},{24,32},{32,40},{40,48},{48,56},{56,64},{64,7... | collective-permute-start | bytes 4616 | tf_op jit(solution)/shard_map/ppermute | solution.py:18
  741.7 12.6 %collective-permute-start.8 = (f32[8,4,128]{2,1,0:T(4,128)S(1)}, f32[8,4,128]{2,1,0:T(4,128)S(1)}, u32[]{:S(2)}, u32[]{:S(2)}) collective-permute-start(f32[8,4,128]{2,1,0:T(4,128)S(1)} %get-tuple-element.302), channel_id=1, source_target_pairs={{0,8},{8,16},{16,24},{24,32},{32,40},{40,48},{48,56},{56,64},{64,7... | collective-permute-start | bytes 49160 | tf_op jit(solution)/shard_map/ppermute | solution.py:26
  744.8 14.0 %collective-permute-start.10 = (f32[8,4,128]{2,1,0:T(4,128)S(1)}, f32[8,4,128]{2,1,0:T(4,128)S(1)}, u32[]{:S(2)}, u32[]{:S(2)}) collective-permute-start(f32[8,4,128]{2,1,0:T(4,128)S(1)} %get-tuple-element.301), channel_id=1, source_target_pairs={{0,120},{8,0},{16,8},{24,16},{32,24},{40,32},{48,40},{56,48},{64,5... | collective-permute-start | bytes 49160 | tf_op jit(solution)/shard_map/ppermute | solution.py:26
  747.4 13.7 %collective-permute-start.12 = (f32[8,4,128]{2,1,0:T(4,128)S(1)}, f32[8,4,128]{2,1,0:T(4,128)S(1)}, u32[]{:S(2)}, u32[]{:S(2)}) collective-permute-start(f32[8,4,128]{2,1,0:T(4,128)S(1)} %get-tuple-element.300), channel_id=1, source_target_pairs={{0,8},{8,16},{16,24},{24,32},{32,40},{40,48},{48,56},{56,64},{64,7... | collective-permute-start | bytes 49160 | tf_op jit(solution)/shard_map/ppermute | solution.py:26
  747.5 15.7 %collective-permute-start.14 = (f32[8,4,128]{2,1,0:T(4,128)S(1)}, f32[8,4,128]{2,1,0:T(4,128)S(1)}, u32[]{:S(2)}, u32[]{:S(2)}) collective-permute-start(f32[8,4,128]{2,1,0:T(4,128)S(1)} %get-tuple-element.299), channel_id=1, source_target_pairs={{0,120},{8,0},{16,8},{24,16},{32,24},{40,32},{48,40},{56,48},{64,5... | collective-permute-start | bytes 49160 | tf_op jit(solution)/shard_map/ppermute | solution.py:26
  752.2 12.8 %collective-permute-start.7 = (f32[8,4,128]{2,1,0:T(4,128)S(1)}, f32[8,4,128]{2,1,0:T(4,128)S(1)}, u32[]{:S(2)}, u32[]{:S(2)}) collective-permute-start(f32[8,4,128]{2,1,0:T(4,128)S(1)} %get-tuple-element.303), channel_id=1, source_target_pairs={{1,0},{2,1},{3,2},{4,3},{5,4},{6,5},{7,6},{9,8},{10,9},{11,10},{12... | collective-permute-start | bytes 49160 | tf_op jit(solution)/shard_map/ppermute | solution.py:32
  754.3 10.8 %collective-permute-start.9 = (f32[8,4,128]{2,1,0:T(4,128)S(1)}, f32[8,4,128]{2,1,0:T(4,128)S(1)}, u32[]{:S(2)}, u32[]{:S(2)}) collective-permute-start(f32[8,4,128]{2,1,0:T(4,128)S(1)} %collective-permute-done.8), channel_id=1, source_target_pairs={{0,1},{1,2},{2,3},{3,4},{4,5},{5,6},{6,7},{8,9},{9,10},{10,11},{11... | collective-permute-start | bytes 49160 | tf_op jit(solution)/shard_map/ppermute | solution.py:32
  758.8 6.4 collective-permute-start.11
  761.2 5.1 collective-permute-start.13
  763.1 5.1 collective-permute-start.15
  768.2 0.7 copy-start.1
where the time goes:
time: 776 us; the launch traced here: 769 us
  other arithmetic  365 us (47%)
  local copies, waits for them, and re-layouts  230 us (30%)
  matrix products  103 us (13%)
  starting transfers between devices  43.9 us (6%)
  waiting for transfers between devices  13.6 us (2%)
  loops' own time  12.7 us (2%)
    gather x48, other arithmetic, one_group(): fcor = jnp.take(coriolis, cells // cells_x, axis=0)  322 us
    gather x32, local copies, waits for them, and re-layouts, one_group(): sample = jnp.take(grad_flat, lvls * ncell + cells, axis=1)  178 us
    dot_general x16, matrix products, one_group(): carry = carry + jnp.dot(weights, onehot, precision=HIGH)  103 us
    gather x32, local copies, waits for them, and re-layouts, one_group(): fcor = jnp.take(coriolis, cells // cells_x, axis=0)  22.6 us
    ppermute x6, starting transfers between devices, passed_along_2(): return lax.ppermute(block, axis, route)  18.2 us
  transfers between devices with their start and end apart: 18, of which 5 were waited for; matrix products, arithmetic and copies ran while one was open for 1% of the time, Pallas kernels for 0%

commit v1 on v0

v1 whole, which is shorter than its diff:
```python
import jax
import jax.numpy as jnp
from jax import lax
from jax.experimental import pallas as pl
from jax.experimental.pallas import tpu as pltpu
from jax.sharding import PartitionSpec as P

STEP = 0.1
DIRS = ((0, 1), (0, -1), (1, 0), (-1, 0), (1, 1), (1, -1), (-1, 1), (-1, -1))
MESH = pl.DeviceIdType.MESH
LEV, CY, CX, NB = 12, 32, 128, 128
ROWS = LEV * CY
GRP = 8
SPAN = GRP * 128
STEPS = NB // GRP
F32, BF16 = jnp.float32, jnp.bfloat16


def propagate(wave_k, wave_l, wave_m, action, sample, fcor, turn):
    new_k = wave_k - STEP * (wave_k * sample[0] + wave_l * sample[1])
    new_l = wave_l - STEP * (wave_k * sample[2] + wave_l * sample[3])
    new_m = wave_m - STEP * (wave_k * sample[4] + wave_l * sample[5])
    new_m = jnp.where(turn == 1, -new_m, new_m)
    horiz = new_k * new_k + new_l * new_l
    total = horiz + new_m * new_m + 1.0
    fsq = fcor * fcor
    freq2 = (horiz + fsq * (new_m * new_m + 1.0)) / total
    freq = jnp.sqrt(freq2)
    group_x = new_k * (1.0 - freq2) / (freq * total)
    group_z = new_m * (fsq - freq2) / (freq * total)
    return (
        new_k,
        new_l,
        new_m,
        group_z * new_k * action,
        group_z * new_l * action,
        group_x * new_k * action,
    )


def level_diff(field):
    zero = jnp.zeros((CY, CX), F32)
    upper = jnp.concatenate([field[CY:], zero], axis=0)
    lower = jnp.concatenate([zero, field[:-CY]], axis=0)
    return (upper - lower) * 0.5


def split(value):
    high = value.astype(BF16)
    return high, (value - high.astype(F32)).astype(BF16)


def kernel(
    leaving, count, fcor, winds, rays, cell, level, turn,
    rays_out, arrived, tend,
    wind_t, table, hots, samples, fluxes, dep,
    lon_out, lon_in, lat_out, lat_in, edge_out, edge_in, box_out, box_in,
    send_sem, recv_sem,
):
    lon, lat = lax.axis_index("lon"), lax.axis_index("lat")
    nlon, nlat = lax.axis_size("lon"), lax.axis_size("lat")

    def at(dlat, dlon):
        return (lax.rem(lon + dlon + nlon, nlon), lax.rem(lat + dlat + nlat, nlat))

    def copy(src, dst, which, where):
        return pltpu.make_async_remote_copy(
            src_ref=src, dst_ref=dst, send_sem=send_sem.at[which], recv_sem=recv_sem.at[which],
            device_id=at(*where), device_id_type=MESH,
        )

    barrier = pltpu.get_barrier_semaphore()
    for where in DIRS:
        pl.semaphore_signal(barrier, inc=1, device_id=at(*where), device_id_type=MESH)

    for w in range(2):
        flipped = winds[w * ROWS : (w + 1) * ROWS, :].T
        wind_t[w] = flipped
        lon_out[0, w : w + 1, :] = flipped[CX - 1 : CX, :]
        lon_out[1, w : w + 1, :] = flipped[0:1, :]
    for half in range(2):
        lon_out[half, 2:8, :] = jnp.zeros((6, ROWS), F32)
    lat_out[0] = winds[pl.ds(CY - 1, 2 * LEV, stride=CY), :]
    lat_out[1] = winds[pl.ds(0, 2 * LEV, stride=CY), :]
    pl.semaphore_wait(barrier, 8)
    halos = [
        copy(lon_out.at[0], lon_in.at[0], 0, (0, 1)),
        copy(lon_out.at[1], lon_in.at[1], 1, (0, -1)),
        copy(lat_out.at[0], lat_in.at[0], 2, (1, 0)),
        copy(lat_out.at[1], lat_in.at[1], 3, (-1, 0)),
    ]
    for each in halos:
        each.start()

    def keep(field, flipped):
        high, low = split(flipped)
        table[field * CX : (field + 1) * CX, 0:ROWS] = high
        table[field * CX : (field + 1) * CX, ROWS : 2 * ROWS] = low

    for w in range(2):
        keep(4 + w, level_diff(winds[w * ROWS : (w + 1) * ROWS, :]).T)
    for each in halos:
        each.wait()

    column = lax.broadcasted_iota(jnp.int32, (CX, ROWS), 0)
    row = lax.rem(lax.broadcasted_iota(jnp.int32, (ROWS, CX), 0), CY)
    for w in range(2):
        flipped = wind_t[w]
        east = jnp.where(column == CX - 1, lon_in[1, w : w + 1, :], pltpu.roll(flipped, CX - 1, 0))
        west = jnp.where(column == 0, lon_in[0, w : w + 1, :], pltpu.roll(flipped, 1, 0))
        keep(w, (east - west) * 0.5)
        field = winds[w * ROWS : (w + 1) * ROWS, :]
        below = jnp.where(lat == 0, 0.0, lat_in[0, w * LEV : (w + 1) * LEV, :])
        above = jnp.where(lat == nlat - 1, 0.0, lat_in[1, w * LEV : (w + 1) * LEV, :])
        spread = lambda edge: jnp.broadcast_to(edge[:, None, :], (LEV, CY, CX)).reshape(ROWS, CX)
        north = jnp.where(row == CY - 1, spread(above), pltpu.roll(field, ROWS - 1, 0))
        south = jnp.where(row == 0, spread(below), pltpu.roll(field, 1, 0))
        keep(2 + w, ((north - south) * 0.5).T)

    x_ids = lax.broadcasted_iota(jnp.int32, (CX, 128), 0)
    r_ids = lax.broadcasted_iota(jnp.int32, (ROWS, 128), 0)

    def gather(c, carry):
        for i in range(GRP):
            cells = cell[pl.ds(c * GRP + i, 1), :]
            rows = level[pl.ds(c * GRP + i, 1), :] * CY + lax.shift_right_logical(cells, 7)
            hots[c, :, i * 128 : (i + 1) * 128] = jnp.where(r_ids == rows, 1.0, 0.0).astype(BF16)
        hot = hots[c]
        picked = lax.dot_general(
            table[...], jnp.concatenate([hot, hot], axis=0), (((1,), (0,)), ((), ())),
            preferred_element_type=F32,
        )
        for i in range(GRP):
            mask = x_ids == jnp.bitwise_and(cell[pl.ds(c * GRP + i, 1), :], CX - 1)
            for f in range(6):
                part = picked[f * CX : (f + 1) * CX, i * 128 : (i + 1) * 128]
                samples[f, i : i + 1, :] = jnp.sum(jnp.where(mask, part, 0.0), axis=0, keepdims=True)
        blocks = pl.ds(pl.multiple_of(c * GRP, GRP), GRP)
        y = lax.shift_right_logical(cell[blocks, :], 7)
        f_ray = jnp.zeros((GRP, 128), F32)
        for i in range(CY):
            f_ray = jnp.where(y == i, fcor[i], f_ray)
        fields = [rays[pl.ds(c * GRP * 4 + f, GRP, stride=4), :] for f in range(4)]
        out = propagate(*fields, [samples[f] for f in range(6)], f_ray, turn[blocks, :])
        for f, value in enumerate((*out[:3], fields[3])):
            rays_out[pl.ds(c * GRP * 4 + f, GRP, stride=4), :] = value
        for j in range(3):
            high = out[3 + j].astype(BF16).astype(F32)
            fluxes[2 * j, blocks, :] = high
            fluxes[2 * j + 1, blocks, :] = out[3 + j] - high
        return carry

    lax.fori_loop(0, STEPS, gather, 0)

    boxes = []
    for d, where in enumerate(DIRS):
        for slot in range(8):
            block = rays_out[pl.ds(leaving[d, slot] * 4, 4), :]
            box_out[d, slot * 4 : slot * 4 + 4, :] = jnp.where(slot < count[d], block, 0.0)
        boxes.append(copy(box_out.at[d], box_in.at[d], 4 + d, where))
        boxes[-1].start()

    def scatter(js):
        first = js[0]
        width = len(js) * 2 * CX

        def step(c, carry):
            parts = []
            for i in range(2 * GRP):
                at_row = pl.ds(c * 2 * GRP + i, 1)
                mask = x_ids == jnp.bitwise_and(cell[at_row, :], CX - 1)
                parts.append(
                    jnp.concatenate(
                        [
                            jnp.where(mask, fluxes[2 * j + p, at_row, :], 0.0).astype(BF16)
                            for j in js
                            for p in range(2)
                        ],
                        axis=0,
                    )
                )
            hot = jnp.concatenate([hots[2 * c], hots[2 * c + 1]], axis=1)
            dep[:, first * 2 * CX : first * 2 * CX + width] += lax.dot_general(
                hot, jnp.concatenate(parts, axis=1), (((1,), (1,)), ((), ())),
                preferred_element_type=F32,
            )
            return carry

        dep[:, first * 2 * CX : first * 2 * CX + width] = jnp.zeros((ROWS, width), F32)
        lax.fori_loop(0, STEPS // 2, step, 0)

    def deposit(j):
        return dep[:, j * 2 * CX : j * 2 * CX + CX] + dep[:, j * 2 * CX + CX : (j + 1) * 2 * CX]

    scatter((2,))
    zonal = deposit(2).T
    wind_t[0] = zonal
    for half in range(2):
        edge_out[half] = jnp.zeros((8, ROWS), F32)
    edge_out[0, 0:1, :] = zonal[CX - 1 : CX, :]
    edge_out[1, 0:1, :] = zonal[0:1, :]
    edges = [
        copy(edge_out.at[0], edge_in.at[0], 12, (0, 1)),
        copy(edge_out.at[1], edge_in.at[1], 13, (0, -1)),
    ]
    for each in edges:
        each.start()
    scatter((0, 1))
    tend[ROWS : 2 * ROWS, :] = -level_diff(deposit(1))
    for each in edges:
        each.wait()
    zonal = wind_t[0]
    east = jnp.where(column == CX - 1, edge_in[1, 0:1, :], pltpu.roll(zonal, CX - 1, 0))
    west = jnp.where(column == 0, edge_in[0, 0:1, :], pltpu.roll(zonal, 1, 0))
    tend[0:ROWS, :] = -level_diff(deposit(0)) - ((east - west) * 0.5).T
    for each in boxes:
        each.wait()
    arrived[...] = box_in[...]


def on_device(winds, coriolis, rays, ray_cell, ray_level, turning, leaving, leave_count):
    vmem = pl.BlockSpec(memory_space=pltpu.VMEM)
    smem = pl.BlockSpec(memory_space=pltpu.SMEM)
    rays_new, arrived, tendency = pl.pallas_call(
        kernel,
        out_shape=(
            jax.ShapeDtypeStruct((NB * 4, 128), F32),
            jax.ShapeDtypeStruct((8, 32, 128), F32),
            jax.ShapeDtypeStruct((2 * ROWS, CX), F32),
        ),
        in_specs=[smem] * 3 + [vmem] * 5,
        out_specs=(vmem, vmem, vmem),
        scratch_shapes=[
            pltpu.VMEM((2, CX, ROWS), F32),
            pltpu.VMEM((6 * CX, 2 * ROWS), BF16),
            pltpu.VMEM((STEPS, ROWS, SPAN), BF16),
            pltpu.VMEM((6, GRP, 128), F32),
            pltpu.VMEM((6, NB, 128), F32),
            pltpu.VMEM((ROWS, 6 * CX), F32),
            pltpu.VMEM((2, 8, ROWS), F32),
            pltpu.VMEM((2, 8, ROWS), F32),
            pltpu.VMEM((2, 2 * LEV, CX), F32),
            pltpu.VMEM((2, 2 * LEV, CX), F32),
            pltpu.VMEM((2, 8, ROWS), F32),
            pltpu.VMEM((2, 8, ROWS), F32),
            pltpu.VMEM((8, 32, 128), F32),
            pltpu.VMEM((8, 32, 128), F32),
            pltpu.SemaphoreType.DMA((14,)),
            pltpu.SemaphoreType.DMA((14,)),
        ],
        compiler_params=pltpu.CompilerParams(
            collective_id=0, has_side_effects=True, vmem_limit_bytes=50 << 20
        ),
        cost_estimate=pl.CostEstimate(flops=30_000_000_000, bytes_accessed=2_000_000, transcendentals=0),
    )(
        leaving.reshape(8, 8),
        leave_count.reshape(8),
        coriolis,
        winds.reshape(2 * ROWS, CX),
        rays.reshape(NB * 4, 128),
        ray_cell.reshape(NB, 128),
        ray_level.reshape(NB, 128),
        turning.reshape(NB, 128),
    )
    return (
        rays_new.reshape(rays.shape),
        arrived.reshape(1, 1, 8, 8, 4, 128),
        tendency.reshape(winds.shape),
    )


def solution(mesh):
    placed = (
        P(None, None, "lat", "lon"),
        P("lat"),
        P("lon", "lat", None, None, None),
        P("lon", "lat", None, None),
        P("lon", "lat", None, None),
        P("lon", "lat", None, None),
        P("lon", "lat", None, None),
        P("lon", "lat", None),
    )
    return jax.shard_map(
        on_device,
        mesh=mesh,
        in_specs=placed,
        out_specs=(
            P("lon", "lat", None, None, None),
            P("lon", "lat", None, None, None, None),
            P(None, None, "lat", "lon"),
        ),
        check_vma=False,
    )
```

time: 776 us -> 59.9 us (0.08)
  other arithmetic: 365 us -> 0 us
  local copies, waits for them, and re-layouts: 230 us -> 7.24 us
  matrix products: 103 us -> 0 us
  Pallas kernels: 0 us -> 51.6 us
  starting transfers between devices: 43.9 us -> 0 us
  waiting for transfers between devices: 13.6 us -> 0 us
  loops' own time: 12.7 us -> 0 us
    gather x65 -> x0, other arithmetic: 322 us -> none  [the longest x48 322 us: one_group(): fcor = jnp.take(coriolis, cells // cells_x, axis=0)]
    gather x65 -> x0, local copies, waits for them, and re-layouts: 202 us -> none  [the longest x32 178 us: one_group(): sample = jnp.take(grad_flat, lvls * ncell + cells, axis=1)]
    dot_general x16 -> x0, matrix products: 103 us -> none  [one_group(): carry = carry + jnp.dot(weights, onehot, precision=HIGH)]
    pallas_call x0 -> x1, Pallas kernels: none -> 51.6 us  [on_device(): pl.pallas_call(kernel, out_shape=(jax.ShapeDtypeStruct((NB * 4, 128), F32...]
    ppermute x18 -> x0, starting transfers between devices: 43.9 us -> none  [the longest x6 18.2 us: passed_along_2(): return lax.ppermute(block, axis, route)]
    mul x65 -> x0, other arithmetic: 16.1 us -> none  [the longest x16 11.1 us: one_group(): sample = jnp.take(grad_flat, lvls * ncell + cells, axis=1)]
    ppermute x18 -> x0, waiting for transfers between devices: 13.6 us -> none  [the longest x3 6.64 us: padded_2(): before = lax.ppermute(last, axis, up)]
    concatenate x1 -> x0, local copies, waits for them, and re-layouts: 12.8 us -> none  [on_device(): jnp.concatenate([(wide_x[..., 2:] - wide_x[..., :-2]) * 0.5, (wide_y[:, :...]
  transfers between devices with their start and end apart: 18 -> 0, of which waited for: 5 -> 0; matrix products, arithmetic and copies ran while one was open for 1% -> 0% of each run, Pallas kernels for 0% -> 0%
where the time goes in v1:
time: 59.9 us; the launch traced here: 59.5 us
  Pallas kernels  51.6 us (86%)
  local copies, waits for them, and re-layouts  7.24 us (12%)
  between operations  0.67 us (1%)
    pallas_call x1, Pallas kernels, on_device(): pl.pallas_call(kernel, out_shape=(jax.ShapeDtypeStruct((NB * 4, 128), F32...  51.6 us
    unnamed x19, local copies, waits for them, and re-layouts  7.24 us

profile of v1, /device:TPU:1, one launch (start us, length us, event | category | flops | bytes accessed | tf_op | source)
XLA Modules:
  0.0 59.5 jit_solution(13146435654047968640)
XLA Ops:
  0.6 0.0 copy-start.5
  0.6 0.0 copy-start.6
  0.7 0.0 copy-start.7
  0.7 0.7 %copy-done.5 = s32[1,1,8,8]{3,2,1,0:T(8,128)S(1)} copy-done((s32[1,1,8,8]{3,2,1,0:T(8,128)S(1)}, s32[1,1,8,8]{3,2,1,0:T(8,128)}, u32[]{:S(2)}) %copy-start.5) | copy-done | bytes 280
  1.3 0.0 copy-done.6
  1.3 0.0 copy-done.7
  1.3 0.0 copy-start
  1.3 1.0 %copy-done = f32[2,12,32,128]{3,2,1,0:T(8,128)S(1)} copy-done((f32[2,12,32,128]{3,2,1,0:T(8,128)S(1)}, f32[2,12,32,128]{3,2,1,0:T(8,128)}, u32[]{:S(2)}) %copy-start) | copy-done | bytes 393240
  2.3 0.0 copy-start.1
  2.3 0.9 %copy-done.1 = f32[1,1,128,4,128]{4,3,2,1,0:T(4,128)S(1)} copy-done((f32[1,1,128,4,128]{4,3,2,1,0:T(4,128)S(1)}, f32[1,1,128,4,128]{4,3,2,1,0:T(4,128)}, u32[]{:S(2)}) %copy-start.1) | copy-done | bytes 262168
  3.3 0.0 copy-start.2
  3.3 0.8 %copy-done.2 = s32[1,1,128,128]{3,2,1,0:T(8,128)S(1)} copy-done((s32[1,1,128,128]{3,2,1,0:T(8,128)S(1)}, s32[1,1,128,128]{3,2,1,0:T(8,128)}, u32[]{:S(2)}) %copy-start.2) | copy-done | bytes 65560
  4.1 0.0 copy-start.3
  4.1 0.8 %copy-done.3 = s32[1,1,128,128]{3,2,1,0:T(8,128)S(1)} copy-done((s32[1,1,128,128]{3,2,1,0:T(8,128)S(1)}, s32[1,1,128,128]{3,2,1,0:T(8,128)}, u32[]{:S(2)}) %copy-start.3) | copy-done | bytes 65560
  5.0 0.0 copy-start.4
  5.0 0.8 %copy-done.4 = s32[1,1,128,128]{3,2,1,0:T(8,128)S(1)} copy-done((s32[1,1,128,128]{3,2,1,0:T(8,128)S(1)}, s32[1,1,128,128]{3,2,1,0:T(8,128)}, u32[]{:S(2)}) %copy-start.4) | copy-done | bytes 65560
  5.8 51.6 %shard_map.103 = (f32[512,128]{1,0:T(8,128)S(1)}, f32[8,32,128]{2,1,0:T(8,128)S(1)}, f32[768,128]{1,0:T(8,128)S(1)}) custom-call(s32[8,8]{1,0:T(8,128)S(1)} %bitcast.18, s32[8]{0:T(128)S(1)} %bitcast.19, f32[32]{0:T(128)S(1)} %copy-done.7, f32[768,128]{1,0:T(8,128)S(1)} %bitcast.13, f32[512,128]{1,0:T(8,128)S(1)} %bitcast.14, s32[128,128]{1,0:T(8,128)S(1)} %bitcast.15, ...), custom_call_target="tpu_custom_call" | custom-call | flops 30000001024 | bytes 2000000 | tf_op jit(solution)/shard_map/pallas_call | solution.py:224
  57.4 0.7 %copy.14 = f32[1,1,128,4,128]{4,3,2,1,0:T(4,128)} copy(f32[1,1,128,4,128]{4,3,2,1,0:T(4,128)S(1)} %bitcast.11) | data formatting | bytes 524288
  58.1 0.7 %copy.15 = f32[1,1,8,8,4,128]{5,4,3,2,1,0:T(4,128)} copy(f32[1,1,8,8,4,128]{5,4,3,2,1,0:T(4,128)S(1)} %bitcast.12) | data formatting | bytes 262144
  58.8 0.7 %copy.16 = f32[2,12,32,128]{3,2,1,0:T(8,128)} copy(f32[2,12,32,128]{3,2,1,0:T(8,128)S(1)} %bitcast.10) | data formatting | bytes 786432
Async XLA Ops:
  0.6 0.7 %copy-start.5 = (s32[1,1,8,8]{3,2,1,0:T(8,128)S(1)}, s32[1,1,8,8]{3,2,1,0:T(8,128)}, u32[]{:S(2)}) copy-start(s32[1,1,8,8]{3,2,1,0:T(8,128)} %param.14) | copy-start | bytes 772
  0.6 0.7 %copy-start.6 = (s32[1,1,8]{2,1,0:T(1,128)S(1)}, s32[1,1,8]{2,1,0:T(1,128)}, u32[]{:S(2)}) copy-start(s32[1,1,8]{2,1,0:T(1,128)} %param.15) | copy-start | bytes 100
  0.7 0.7 %copy-start.7 = (f32[32]{0:T(128)S(1)}, f32[32]{0:T(128)}, u32[]{:S(2)}) copy-start(f32[32]{0:T(128)} %fcor.1) | copy-start | bytes 388
  1.3 1.0 %copy-start = (f32[2,12,32,128]{3,2,1,0:T(8,128)S(1)}, f32[2,12,32,128]{3,2,1,0:T(8,128)}, u32[]{:S(2)}) copy-start(f32[2,12,32,128]{3,2,1,0:T(8,128)} %param.8) | copy-start | bytes 1179652
  2.3 0.9 %copy-start.1 = (f32[1,1,128,4,128]{4,3,2,1,0:T(4,128)S(1)}, f32[1,1,128,4,128]{4,3,2,1,0:T(4,128)}, u32[]{:S(2)}) copy-start(f32[1,1,128,4,128]{4,3,2,1,0:T(4,128)} %param.10) | copy-start | bytes 786436
  3.3 0.8 %copy-start.2 = (s32[1,1,128,128]{3,2,1,0:T(8,128)S(1)}, s32[1,1,128,128]{3,2,1,0:T(8,128)}, u32[]{:S(2)}) copy-start(s32[1,1,128,128]{3,2,1,0:T(8,128)} %param.11) | copy-start | bytes 196612
  4.1 0.8 %copy-start.3 = (s32[1,1,128,128]{3,2,1,0:T(8,128)S(1)}, s32[1,1,128,128]{3,2,1,0:T(8,128)}, u32[]{:S(2)}) copy-start(s32[1,1,128,128]{3,2,1,0:T(8,128)} %param.12) | copy-start | bytes 196612
  5.0 0.8 %copy-start.4 = (s32[1,1,128,128]{3,2,1,0:T(8,128)S(1)}, s32[1,1,128,128]{3,2,1,0:T(8,128)}, u32[]{:S(2)}) copy-start(s32[1,1,128,128]{3,2,1,0:T(8,128)} %param.13) | copy-start | bytes 196612

commit v2 on v1

--- a/solution.py
+++ b/solution.py
@@ -13,6 +13,7 @@
 GRP = 8
 SPAN = GRP * 128
 STEPS = NB // GRP
+UNIT = 5461.0
 F32, BF16 = jnp.float32, jnp.bfloat16
 
 
@@ -50,13 +51,43 @@
     return high, (value - high.astype(F32)).astype(BF16)
 
 
+def pack(first, second):
+    high = jnp.round(first * UNIT).astype(jnp.int32)
+    low = jnp.round(second * UNIT).astype(jnp.int32)
+    return high * 65536 + (low + 32768)
+
+
+def unpack(word):
+    high = lax.shift_right_arithmetic(word, 16)
+    low = jnp.bitwise_and(word, 65535) - 32768
+    return high.astype(F32) * (1.0 / UNIT), low.astype(F32) * (1.0 / UNIT)
+
+
 def kernel(
+    leaving_in, count_in, fcor_in, winds_in, rays_in, cell_in, level_in, turn_in,
+    rays_out, arrived, tend,
     leaving, count, fcor, winds, rays, cell, level, turn,
-    rays_out, arrived, tend,
-    wind_t, table, hots, samples, fluxes, dep,
+    wind_t, table, words, hots, samples, fluxes, dep,
     lon_out, lon_in, lat_out, lat_in, edge_out, edge_in, box_out, box_in,
-    send_sem, recv_sem,
+    load_sem, send_sem, recv_sem,
 ):
+    loads = [
+        pltpu.make_async_copy(src, dst, load_sem.at[i])
+        for i, (src, dst) in enumerate(
+            (
+                (winds_in, winds),
+                (cell_in, cell),
+                (level_in, level),
+                (rays_in, rays),
+                (turn_in, turn),
+                (fcor_in, fcor),
+                (leaving_in, leaving),
+                (count_in, count),
+            )
+        )
+    ]
+    for each in loads:
+        each.start()
     lon, lat = lax.axis_index("lon"), lax.axis_index("lat")
     nlon, nlat = lax.axis_size("lon"), lax.axis_size("lat")
 
@@ -73,6 +104,7 @@
     for where in DIRS:
         pl.semaphore_signal(barrier, inc=1, device_id=at(*where), device_id_type=MESH)
 
+    loads[0].wait()
     for w in range(2):
         flipped = winds[w * ROWS : (w + 1) * ROWS, :].T
         wind_t[w] = flipped
@@ -98,59 +130,104 @@
         table[field * CX : (field + 1) * CX, ROWS : 2 * ROWS] = low
 
     for w in range(2):
-        keep(4 + w, level_diff(winds[w * ROWS : (w + 1) * ROWS, :]).T)
+        keep(w, level_diff(winds[w * ROWS : (w + 1) * ROWS, :]).T)
+    hots[0] = jnp.zeros((ROWS, SPAN), BF16)
+    fluxes[:, 0:GRP, :] = jnp.zeros((6, GRP, 128), F32)
+    dep[...] = jnp.zeros((ROWS, 6 * CX), F32)
     for each in halos:
         each.wait()
 
     column = lax.broadcasted_iota(jnp.int32, (CX, ROWS), 0)
     row = lax.rem(lax.broadcasted_iota(jnp.int32, (ROWS, CX), 0), CY)
+    along, across = [], []
     for w in range(2):
         flipped = wind_t[w]
         east = jnp.where(column == CX - 1, lon_in[1, w : w + 1, :], pltpu.roll(flipped, CX - 1, 0))
         west = jnp.where(column == 0, lon_in[0, w : w + 1, :], pltpu.roll(flipped, 1, 0))
-        keep(w, (east - west) * 0.5)
+        along.append((east - west) * 0.5)
         field = winds[w * ROWS : (w + 1) * ROWS, :]
         below = jnp.where(lat == 0, 0.0, lat_in[0, w * LEV : (w + 1) * LEV, :])
         above = jnp.where(lat == nlat - 1, 0.0, lat_in[1, w * LEV : (w + 1) * LEV, :])
         spread = lambda edge: jnp.broadcast_to(edge[:, None, :], (LEV, CY, CX)).reshape(ROWS, CX)
         north = jnp.where(row == CY - 1, spread(above), pltpu.roll(field, ROWS - 1, 0))
         south = jnp.where(row == 0, spread(below), pltpu.roll(field, 1, 0))
-        keep(2 + w, ((north - south) * 0.5).T)
+        across.append((north - south) * 0.5)
+    words[0] = pack(*along).T
+    words[1] = pack(*across)
+    for each in loads[1:]:
+        each.wait()
 
     x_ids = lax.broadcasted_iota(jnp.int32, (CX, 128), 0)
     r_ids = lax.broadcasted_iota(jnp.int32, (ROWS, 128), 0)
 
-    def gather(c, carry):
+    def gather(c):
         for i in range(GRP):
             cells = cell[pl.ds(c * GRP + i, 1), :]
             rows = level[pl.ds(c * GRP + i, 1), :] * CY + lax.shift_right_logical(cells, 7)
-            hots[c, :, i * 128 : (i + 1) * 128] = jnp.where(r_ids == rows, 1.0, 0.0).astype(BF16)
-        hot = hots[c]
+            hots[c + 1, :, i * 128 : (i + 1) * 128] = jnp.where(r_ids == rows, 1.0, 0.0).astype(BF16)
+        hot = hots[c + 1]
         picked = lax.dot_general(
             table[...], jnp.concatenate([hot, hot], axis=0), (((1,), (0,)), ((), ())),
             preferred_element_type=F32,
         )
         for i in range(GRP):
             mask = x_ids == jnp.bitwise_and(cell[pl.ds(c * GRP + i, 1), :], CX - 1)
-            for f in range(6):
+            for f in range(2):
                 part = picked[f * CX : (f + 1) * CX, i * 128 : (i + 1) * 128]
                 samples[f, i : i + 1, :] = jnp.sum(jnp.where(mask, part, 0.0), axis=0, keepdims=True)
         blocks = pl.ds(pl.multiple_of(c * GRP, GRP), GRP)
-        y = lax.shift_right_logical(cell[blocks, :], 7)
+        cells = cell[blocks, :]
+        x = jnp.bitwise_and(cells, CX - 1)
+        y = lax.shift_right_logical(cells, 7)
+        rows = level[blocks, :] * CY + y
+        found = [jnp.zeros((GRP, 128), jnp.int32)] * 2
+        for r in range(ROWS):
+            here = rows == r
+            for w in range(2):
+                line = jnp.broadcast_to(words[w, r : r + 1, :], (GRP, CX))
+                got = jnp.take_along_axis(line, x, axis=1, mode="promise_in_bounds")
+                found[w] = jnp.where(here, got, found[w])
         f_ray = jnp.zeros((GRP, 128), F32)
         for i in range(CY):
             f_ray = jnp.where(y == i, fcor[i], f_ray)
         fields = [rays[pl.ds(c * GRP * 4 + f, GRP, stride=4), :] for f in range(4)]
-        out = propagate(*fields, [samples[f] for f in range(6)], f_ray, turn[blocks, :])
+        sample = (*unpack(found[0]), *unpack(found[1]), samples[0], samples[1])
+        out = propagate(*fields, sample, f_ray, turn[blocks, :])
         for f, value in enumerate((*out[:3], fields[3])):
             rays_out[pl.ds(c * GRP * 4 + f, GRP, stride=4), :] = value
+        after = pl.ds(pl.multiple_of(c * GRP + GRP, GRP), GRP)
         for j in range(3):
             high = out[3 + j].astype(BF16).astype(F32)
-            fluxes[2 * j, blocks, :] = high
-            fluxes[2 * j + 1, blocks, :] = out[3 + j] - high
+            fluxes[2 * j, after, :] = high
+            fluxes[2 * j + 1, after, :] = out[3 + j] - high
+
+    def scatter(js, c, steps):
+        parts = []
+        for i in range(steps * GRP):
+            mask = x_ids == jnp.bitwise_and(cell[pl.ds(jnp.maximum(c * GRP, 0) + i, 1), :], CX - 1)
+            parts.append(
+                jnp.concatenate(
+                    [
+                        jnp.where(mask, fluxes[2 * j + p, pl.ds(c * GRP + GRP + i, 1), :], 0.0).astype(BF16)
+                        for j in js
+                        for p in range(2)
+                    ],
+                    axis=0,
+                )
+            )
+        hot = jnp.concatenate([hots[c + 1 + i] for i in range(steps)], axis=1)
+        lanes = slice(js[0] * 2 * CX, (js[-1] + 1) * 2 * CX)
+        dep[:, lanes] += lax.dot_general(
+            hot, jnp.concatenate(parts, axis=1), (((1,), (1,)), ((), ())),
+            preferred_element_type=F32,
+        )
+
+    def both(c, carry):
+        scatter((1, 2), c - 1, 1)
+        gather(c)
         return carry
 
-    lax.fori_loop(0, STEPS, gather, 0)
+    lax.fori_loop(0, STEPS, both, 0)
 
     boxes = []
     for d, where in enumerate(DIRS):
@@ -160,39 +237,10 @@
         boxes.append(copy(box_out.at[d], box_in.at[d], 4 + d, where))
         boxes[-1].start()
 
-    def scatter(js):
-        first = js[0]
-        width = len(js) * 2 * CX
-
-        def step(c, carry):
-            parts = []
-            for i in range(2 * GRP):
-                at_row = pl.ds(c * 2 * GRP + i, 1)
-                mask = x_ids == jnp.bitwise_and(cell[at_row, :], CX - 1)
-                parts.append(
-                    jnp.concatenate(
-                        [
-                            jnp.where(mask, fluxes[2 * j + p, at_row, :], 0.0).astype(BF16)
-                            for j in js
-                            for p in range(2)
-                        ],
-                        axis=0,
-                    )
-                )
-            hot = jnp.concatenate([hots[2 * c], hots[2 * c + 1]], axis=1)
-            dep[:, first * 2 * CX : first * 2 * CX + width] += lax.dot_general(
-                hot, jnp.concatenate(parts, axis=1), (((1,), (1,)), ((), ())),
-                preferred_element_type=F32,
-            )
-            return carry
-
-        dep[:, first * 2 * CX : first * 2 * CX + width] = jnp.zeros((ROWS, width), F32)
-        lax.fori_loop(0, STEPS // 2, step, 0)
-
     def deposit(j):
         return dep[:, j * 2 * CX : j * 2 * CX + CX] + dep[:, j * 2 * CX + CX : (j + 1) * 2 * CX]
 
-    scatter((2,))
+    scatter((1, 2), STEPS - 1, 1)
     zonal = deposit(2).T
     wind_t[0] = zonal
     for half in range(2):
@@ -205,7 +253,7 @@
     ]
     for each in edges:
         each.start()
-    scatter((0, 1))
+    lax.fori_loop(0, STEPS // 2, lambda c, carry: (scatter((0,), 2 * c, 2), carry)[1], 0)
     tend[ROWS : 2 * ROWS, :] = -level_diff(deposit(1))
     for each in edges:
         each.wait()
@@ -220,7 +268,7 @@
 
 def on_device(winds, coriolis, rays, ray_cell, ray_level, turning, leaving, leave_count):
     vmem = pl.BlockSpec(memory_space=pltpu.VMEM)
-    smem = pl.BlockSpec(memory_space=pltpu.SMEM)
+    hbm = pl.BlockSpec(memory_space=pltpu.HBM)
     rays_new, arrived, tendency = pl.pallas_call(
         kernel,
         out_shape=(
@@ -228,14 +276,23 @@
             jax.ShapeDtypeStruct((8, 32, 128), F32),
             jax.ShapeDtypeStruct((2 * ROWS, CX), F32),
         ),
-        in_specs=[smem] * 3 + [vmem] * 5,
+        in_specs=[hbm] * 8,
         out_specs=(vmem, vmem, vmem),
         scratch_shapes=[
+            pltpu.SMEM((8, 8), jnp.int32),
+            pltpu.SMEM((8,), jnp.int32),
+            pltpu.SMEM((32,), F32),
+            pltpu.VMEM((2 * ROWS, CX), F32),
+            pltpu.VMEM((NB * 4, 128), F32),
+            pltpu.VMEM((NB, 128), jnp.int32),
+            pltpu.VMEM((NB, 128), jnp.int32),
+            pltpu.VMEM((NB, 128), jnp.int32),
             pltpu.VMEM((2, CX, ROWS), F32),
-            pltpu.VMEM((6 * CX, 2 * ROWS), BF16),
-            pltpu.VMEM((STEPS, ROWS, SPAN), BF16),
-            pltpu.VMEM((6, GRP, 128), F32),
-            pltpu.VMEM((6, NB, 128), F32),
+            pltpu.VMEM((2 * CX, 2 * ROWS), BF16),
+            pltpu.VMEM((2, ROWS, CX), jnp.int32),
+            pltpu.VMEM((STEPS + 1, ROWS, SPAN), BF16),
+            pltpu.VMEM((2, GRP, 128), F32),
+            pltpu.VMEM((6, NB + GRP, 128), F32),
             pltpu.VMEM((ROWS, 6 * CX), F32),
             pltpu.VMEM((2, 8, ROWS), F32),
             pltpu.VMEM((2, 8, ROWS), F32),
@@ -245,11 +302,12 @@
             pltpu.VMEM((2, 8, ROWS), F32),
             pltpu.VMEM((8, 32, 128), F32),
             pltpu.VMEM((8, 32, 128), F32),
+            pltpu.SemaphoreType.DMA((8,)),
             pltpu.SemaphoreType.DMA((14,)),
             pltpu.SemaphoreType.DMA((14,)),
         ],
         compiler_params=pltpu.CompilerParams(
-            collective_id=0, has_side_effects=True, vmem_limit_bytes=50 << 20
+            collective_id=0, has_side_effects=True, vmem_limit_bytes=62 << 20
         ),
         cost_estimate=pl.CostEstimate(flops=30_000_000_000, bytes_accessed=2_000_000, transcendentals=0),
     )(

time: 59.9 us -> 42.7 us (0.71)
  Pallas kernels: 51.6 us -> 38.8 us
  local copies, waits for them, and re-layouts: 7.24 us -> 3.14 us
    pallas_call x1, Pallas kernels: 51.6 us -> 38.8 us  [on_device(): pl.pallas_call(kernel, out_shape=(jax.ShapeDtypeStruct((NB * 4, 128), F32...]
    unnamed x19 -> x7, local copies, waits for them, and re-layouts: 7.24 us -> 3.14 us
where the time goes in v2:
time: 42.7 us; the launch traced here: 42.6 us
  Pallas kernels  38.8 us (91%)
  local copies, waits for them, and re-layouts  3.14 us (7%)
  between operations  0.66 us (2%)
    pallas_call x1, Pallas kernels, on_device(): pl.pallas_call(kernel, out_shape=(jax.ShapeDtypeStruct((NB * 4, 128), F32...  38.8 us
    unnamed x7, local copies, waits for them, and re-layouts  3.14 us

profile of v2, /device:TPU:1, one launch (start us, length us, event | category | flops | bytes accessed | tf_op | source)
XLA Modules:
  0.0 42.6 jit_solution(14216376654556968779)
XLA Ops:
  0.6 38.8 %shard_map.103 = (f32[512,128]{1,0:T(8,128)}, f32[8,32,128]{2,1,0:T(8,128)}, f32[768,128]{1,0:T(8,128)}) custom-call(s32[8,8]{1,0:T(8,128)} %bitcast.18, s32[8]{0:T(128)} %bitcast.19, f32[32]{0:T(128)} %fcor_in.1, f32[768,128]{1,0:T(8,128)} %bitcast.13, f32[512,128]{1,0:T(8,128)} %bitcast.14, s32[128,128]{1,0:T(8,128)} %bitcast.15, s32[128,128]{1,0:T(8,128)} %bitcast.16, ...), custom_call_target="tpu_custom_call" | custom-call | flops 30000001024 | bytes 2000000 | tf_op jit(solution)/shard_map/pallas_call | solution.py:272
  39.4 0.0 copy-start.1
  39.4 0.0 copy-start
  39.4 1.7 %copy.14 = f32[1,1,128,4,128]{4,3,2,1,0:T(4,128)} copy(f32[1,1,128,4,128]{4,3,2,1,0:T(4,128)} %bitcast.11) | data formatting | bytes 524288
  41.1 0.0 copy-done.1
  41.2 0.7 %copy.15 = f32[1,1,8,8,4,128]{5,4,3,2,1,0:T(4,128)} copy(f32[1,1,8,8,4,128]{5,4,3,2,1,0:T(4,128)S(1)} %bitcast.12) | data formatting | bytes 262144
  41.8 0.0 copy-done
  41.8 0.7 %copy.16 = f32[2,12,32,128]{3,2,1,0:T(8,128)} copy(f32[2,12,32,128]{3,2,1,0:T(8,128)S(1)} %bitcast.10) | data formatting | bytes 786432
Async XLA Ops:
  39.4 1.7 %copy-start.1 = (f32[8,32,128]{2,1,0:T(8,128)S(1)}, f32[8,32,128]{2,1,0:T(8,128)}, u32[]{:S(2)}) copy-start(f32[8,32,128]{2,1,0:T(8,128)} %get-tuple-element.7) | copy-start | bytes 393220
  39.4 2.4 %copy-start = (f32[768,128]{1,0:T(8,128)S(1)}, f32[768,128]{1,0:T(8,128)}, u32[]{:S(2)}) copy-start(f32[768,128]{1,0:T(8,128)} %get-tuple-element.8) | copy-start | bytes 1179652

commit v3 on v2

--- a/solution.py
+++ b/solution.py
@@ -10,6 +10,8 @@
 MESH = pl.DeviceIdType.MESH
 LEV, CY, CX, NB = 12, 32, 128, 128
 ROWS = LEV * CY
+LOW = 128
+LAG = 4
 GRP = 8
 SPAN = GRP * 128
 STEPS = NB // GRP
@@ -67,7 +69,7 @@
     leaving_in, count_in, fcor_in, winds_in, rays_in, cell_in, level_in, turn_in,
     rays_out, arrived, tend,
     leaving, count, fcor, winds, rays, cell, level, turn,
-    wind_t, table, words, hots, samples, fluxes, dep,
+    wind_t, table, words, lat_edge, lon_edge, fresh, hots, found, samples, fluxes, dep,
     lon_out, lon_in, lat_out, lat_in, edge_out, edge_in, box_out, box_in,
     load_sem, send_sem, recv_sem,
 ):
@@ -126,108 +128,165 @@
 
     def keep(field, flipped):
         high, low = split(flipped)
-        table[field * CX : (field + 1) * CX, 0:ROWS] = high
-        table[field * CX : (field + 1) * CX, ROWS : 2 * ROWS] = low
+        lines = slice(field * CX, (field + 1) * CX)
+        table[lines, 0:LOW] = high[:, :LOW]
+        table[lines, LOW : 2 * LOW] = low[:, :LOW]
+        table[lines, 2 * LOW : ROWS + LOW] = high[:, LOW:]
+        table[lines, ROWS + LOW : 2 * ROWS] = low[:, LOW:]
 
     for w in range(2):
         keep(w, level_diff(winds[w * ROWS : (w + 1) * ROWS, :]).T)
-    hots[0] = jnp.zeros((ROWS, SPAN), BF16)
-    fluxes[:, 0:GRP, :] = jnp.zeros((6, GRP, 128), F32)
-    dep[...] = jnp.zeros((ROWS, 6 * CX), F32)
-    for each in halos:
-        each.wait()
-
     column = lax.broadcasted_iota(jnp.int32, (CX, ROWS), 0)
     row = lax.rem(lax.broadcasted_iota(jnp.int32, (ROWS, CX), 0), CY)
+    lane = lax.broadcasted_iota(jnp.int32, (ROWS, CX), 1)
     along, across = [], []
     for w in range(2):
-        flipped = wind_t[w]
-        east = jnp.where(column == CX - 1, lon_in[1, w : w + 1, :], pltpu.roll(flipped, CX - 1, 0))
-        west = jnp.where(column == 0, lon_in[0, w : w + 1, :], pltpu.roll(flipped, 1, 0))
+        field = winds[w * ROWS : (w + 1) * ROWS, :]
+        east = jnp.where(lane == CX - 1, 0.0, pltpu.roll(field, CX - 1, 1))
+        west = jnp.where(lane == 0, 0.0, pltpu.roll(field, 1, 1))
         along.append((east - west) * 0.5)
-        field = winds[w * ROWS : (w + 1) * ROWS, :]
-        below = jnp.where(lat == 0, 0.0, lat_in[0, w * LEV : (w + 1) * LEV, :])
-        above = jnp.where(lat == nlat - 1, 0.0, lat_in[1, w * LEV : (w + 1) * LEV, :])
-        spread = lambda edge: jnp.broadcast_to(edge[:, None, :], (LEV, CY, CX)).reshape(ROWS, CX)
-        north = jnp.where(row == CY - 1, spread(above), pltpu.roll(field, ROWS - 1, 0))
-        south = jnp.where(row == 0, spread(below), pltpu.roll(field, 1, 0))
+        north = jnp.where(row == CY - 1, 0.0, pltpu.roll(field, ROWS - 1, 0))
+        south = jnp.where(row == 0, 0.0, pltpu.roll(field, 1, 0))
         across.append((north - south) * 0.5)
-    words[0] = pack(*along).T
+    words[0] = pack(*along)
     words[1] = pack(*across)
+    words[2] = pack(*[level_diff(winds[w * ROWS : (w + 1) * ROWS, :]) for w in range(2)])
+    dep[...] = jnp.zeros((ROWS, 6 * CX), F32)
     for each in loads[1:]:
         each.wait()
 
     x_ids = lax.broadcasted_iota(jnp.int32, (CX, 128), 0)
     r_ids = lax.broadcasted_iota(jnp.int32, (ROWS, 128), 0)
 
-    def gather(c):
+    def blocks_of(c):
+        return pl.ds(pl.multiple_of(c * GRP, GRP), GRP)
+
+    def place(c):
+        cells = cell[blocks_of(c), :]
+        y = lax.shift_right_logical(cells, 7)
+        return jnp.bitwise_and(cells, CX - 1), y, level[blocks_of(c), :] * CY + y
+
+    def rise(c, whole):
         for i in range(GRP):
             cells = cell[pl.ds(c * GRP + i, 1), :]
             rows = level[pl.ds(c * GRP + i, 1), :] * CY + lax.shift_right_logical(cells, 7)
-            hots[c + 1, :, i * 128 : (i + 1) * 128] = jnp.where(r_ids == rows, 1.0, 0.0).astype(BF16)
-        hot = hots[c + 1]
+            hot = jnp.where(r_ids == rows, 1.0, 0.0).astype(BF16)
+            fresh[:, i * 128 : (i + 1) * 128] = hot
+            hots[c, :, i * 128 : (i + 1) * 128] = hot
+        first, rest = fresh[:LOW, :], fresh[LOW:, :]
         picked = lax.dot_general(
-            table[...], jnp.concatenate([hot, hot], axis=0), (((1,), (0,)), ((), ())),
+            table[...] if whole else table[:, 2 * LOW :],
+            jnp.concatenate([first, first, rest, rest] if whole else [rest, rest], axis=0),
+            (((1,), (0,)), ((), ())),
             preferred_element_type=F32,
         )
         for i in range(GRP):
             mask = x_ids == jnp.bitwise_and(cell[pl.ds(c * GRP + i, 1), :], CX - 1)
             for f in range(2):
                 part = picked[f * CX : (f + 1) * CX, i * 128 : (i + 1) * 128]
-                samples[f, i : i + 1, :] = jnp.sum(jnp.where(mask, part, 0.0), axis=0, keepdims=True)
-        blocks = pl.ds(pl.multiple_of(c * GRP, GRP), GRP)
-        cells = cell[blocks, :]
-        x = jnp.bitwise_and(cells, CX - 1)
-        y = lax.shift_right_logical(cells, 7)
-        rows = level[blocks, :] * CY + y
-        found = [jnp.zeros((GRP, 128), jnp.int32)] * 2
+                samples[f, pl.ds(c * GRP + i, 1), :] = jnp.sum(
+                    jnp.where(mask, part, 0.0), axis=0, keepdims=True
+                )
+
+    def pick(c, whole):
+        x, _, rows = place(c)
+        nought = jnp.full((GRP, 128), 32768, jnp.int32)
+        got = [nought] * 3
         for r in range(ROWS):
             here = rows == r
-            for w in range(2):
+            for w in range(2 if whole or r >= LOW else 3):
                 line = jnp.broadcast_to(words[w, r : r + 1, :], (GRP, CX))
-                got = jnp.take_along_axis(line, x, axis=1, mode="promise_in_bounds")
-                found[w] = jnp.where(here, got, found[w])
+                taken = jnp.take_along_axis(line, x, axis=1, mode="promise_in_bounds")
+                got[w] = jnp.where(here, taken, got[w])
+        for w in range(3):
+            found[w, blocks_of(c), :] = got[w]
+
+    def advance(c):
+        x, y, rows = place(c)
+        levels = level[blocks_of(c), :]
+        sample = [*unpack(found[0, blocks_of(c), :]), *unpack(found[1, blocks_of(c), :])]
+        for f, value in enumerate(unpack(found[2, blocks_of(c), :])):
+            sample.append(value + samples[f, blocks_of(c), :])
+        lanes, tiles = jnp.bitwise_and(rows, 127), lax.shift_right_logical(rows, 7)
+        nought = jnp.full((GRP, 128), 32768, jnp.int32)
+        for side, end in ((0, 0), (1, CX - 1)):
+            word = nought
+            for t in range(ROWS // 128):
+                line = jnp.broadcast_to(lon_edge[side, t : t + 1, :], (GRP, 128))
+                taken = jnp.take_along_axis(line, lanes, axis=1, mode="promise_in_bounds")
+                word = jnp.where(jnp.logical_and(tiles == t, x == end), taken, word)
+            for f, value in enumerate(unpack(word)):
+                sample[f] += value
+        for side, end in ((0, 0), (1, CY - 1)):
+            word = nought
+            for z in range(LEV):
+                line = jnp.broadcast_to(lat_edge[side, z : z + 1, :], (GRP, 128))
+                taken = jnp.take_along_axis(line, x, axis=1, mode="promise_in_bounds")
+                word = jnp.where(jnp.logical_and(levels == z, y == end), taken, word)
+            for f, value in enumerate(unpack(word)):
+                sample[2 + f] += value
         f_ray = jnp.zeros((GRP, 128), F32)
         for i in range(CY):
             f_ray = jnp.where(y == i, fcor[i], f_ray)
         fields = [rays[pl.ds(c * GRP * 4 + f, GRP, stride=4), :] for f in range(4)]
-        sample = (*unpack(found[0]), *unpack(found[1]), samples[0], samples[1])
-        out = propagate(*fields, sample, f_ray, turn[blocks, :])
+        out = propagate(*fields, sample, f_ray, turn[blocks_of(c), :])
         for f, value in enumerate((*out[:3], fields[3])):
             rays_out[pl.ds(c * GRP * 4 + f, GRP, stride=4), :] = value
-        after = pl.ds(pl.multiple_of(c * GRP + GRP, GRP), GRP)
         for j in range(3):
             high = out[3 + j].astype(BF16).astype(F32)
-            fluxes[2 * j, after, :] = high
-            fluxes[2 * j + 1, after, :] = out[3 + j] - high
-
-    def scatter(js, c, steps):
+            fluxes[2 * j, blocks_of(c), :] = high
+            fluxes[2 * j + 1, blocks_of(c), :] = out[3 + j] - high
+
+    def scatter(js, c, hot):
         parts = []
-        for i in range(steps * GRP):
-            mask = x_ids == jnp.bitwise_and(cell[pl.ds(jnp.maximum(c * GRP, 0) + i, 1), :], CX - 1)
+        for i in range(len(hot) * GRP):
+            at_row = pl.ds(c * GRP + i, 1)
+            mask = x_ids == jnp.bitwise_and(cell[at_row, :], CX - 1)
             parts.append(
                 jnp.concatenate(
                     [
-                        jnp.where(mask, fluxes[2 * j + p, pl.ds(c * GRP + GRP + i, 1), :], 0.0).astype(BF16)
+                        jnp.where(mask, fluxes[2 * j + p, at_row, :], 0.0).astype(BF16)
                         for j in js
                         for p in range(2)
                     ],
                     axis=0,
                 )
             )
-        hot = jnp.concatenate([hots[c + 1 + i] for i in range(steps)], axis=1)
         lanes = slice(js[0] * 2 * CX, (js[-1] + 1) * 2 * CX)
         dep[:, lanes] += lax.dot_general(
-            hot, jnp.concatenate(parts, axis=1), (((1,), (1,)), ((), ())),
+            jnp.concatenate(hot, axis=1), jnp.concatenate(parts, axis=1), (((1,), (1,)), ((), ())),
             preferred_element_type=F32,
         )
 
-    def both(c, carry):
-        scatter((1, 2), c - 1, 1)
-        gather(c)
+    def before(c, carry):
+        rise(c, True)
+        pick(c, True)
         return carry
 
-    lax.fori_loop(0, STEPS, both, 0)
+    lax.fori_loop(0, LAG, before, 0)
+
+    for each in halos:
+        each.wait()
+    for side, sign in ((0, -0.5), (1, 0.5)):
+        ends = [lon_in[side, w : w + 1, :] * sign for w in range(2)]
+        word = pack(*ends)
+        for t in range(ROWS // 128):
+            lon_edge[side, t : t + 1, :] = word[:, t * 128 : (t + 1) * 128]
+        closed = lat == (0 if side == 0 else nlat - 1)
+        lat_edge[side] = pack(
+            *[jnp.where(closed, 0.0, lat_in[side, w * LEV : (w + 1) * LEV, :] * sign) for w in range(2)]
+        )
+    advance(0)
+
+    def after(c, carry):
+        scatter((0, 1, 2), c - LAG, [hots[c - LAG]])
+        advance(c - LAG + 1)
+        pick(c, False)
+        rise(c, False)
+        return carry
+
+    lax.fori_loop(LAG, STEPS, after, 0)
+    lax.fori_loop(STEPS - LAG + 1, STEPS, lambda c, carry: (advance(c), carry)[1], 0)
 
     boxes = []
     for d, where in enumerate(DIRS):
@@ -240,7 +299,15 @@
     def deposit(j):
         return dep[:, j * 2 * CX : j * 2 * CX + CX] + dep[:, j * 2 * CX + CX : (j + 1) * 2 * CX]
 
-    scatter((1, 2), STEPS - 1, 1)
+
+    def last(js, first, count):
+        def step(c, carry):
+            scatter(js, first + 2 * c, [hots[first + 2 * c], hots[first + 2 * c + 1]])
+            return carry
+
+        lax.fori_loop(0, count // 2, step, 0)
+
+    last((2,), STEPS - LAG, LAG)
     zonal = deposit(2).T
     wind_t[0] = zonal
     for half in range(2):
@@ -253,7 +320,7 @@
     ]
     for each in edges:
         each.start()
-    lax.fori_loop(0, STEPS // 2, lambda c, carry: (scatter((0,), 2 * c, 2), carry)[1], 0)
+    last((0, 1), STEPS - LAG, LAG)
     tend[ROWS : 2 * ROWS, :] = -level_diff(deposit(1))
     for each in edges:
         each.wait()
@@ -289,10 +356,14 @@
             pltpu.VMEM((NB, 128), jnp.int32),
             pltpu.VMEM((2, CX, ROWS), F32),
             pltpu.VMEM((2 * CX, 2 * ROWS), BF16),
-            pltpu.VMEM((2, ROWS, CX), jnp.int32),
-            pltpu.VMEM((STEPS + 1, ROWS, SPAN), BF16),
-            pltpu.VMEM((2, GRP, 128), F32),
-            pltpu.VMEM((6, NB + GRP, 128), F32),
+            pltpu.VMEM((3, ROWS, CX), jnp.int32),
+            pltpu.VMEM((2, LEV, CX), jnp.int32),
+            pltpu.VMEM((2, ROWS // 128, 128), jnp.int32),
+            pltpu.VMEM((ROWS, SPAN), BF16),
+            pltpu.VMEM((STEPS, ROWS, SPAN), BF16),
+            pltpu.VMEM((3, NB, 128), jnp.int32),
+            pltpu.VMEM((2, NB, 128), F32),
+            pltpu.VMEM((6, NB, 128), F32),
             pltpu.VMEM((ROWS, 6 * CX), F32),
             pltpu.VMEM((2, 8, ROWS), F32),
             pltpu.VMEM((2, 8, ROWS), F32),

time: 42.7 us -> 41.4 us (0.970); the launches traced: 42.6 us -> 40.6 us
  Pallas kernels: 38.8 us -> 36.8 us
    pallas_call x1, Pallas kernels: 38.8 us -> 36.8 us  [on_device(): pl.pallas_call(kernel, out_shape=(jax.ShapeDtypeStruct((NB * 4, 128), F32...]
where the time goes in v3:
time: 41.4 us; the launch traced here: 40.6 us
  Pallas kernels  36.8 us (89%)
  local copies, waits for them, and re-layouts  3.14 us (8%)
  between operations  0.66 us (2%)
    pallas_call x1, Pallas kernels, on_device(): pl.pallas_call(kernel, out_shape=(jax.ShapeDtypeStruct((NB * 4, 128), F32...  36.8 us
    unnamed x7, local copies, waits for them, and re-layouts  3.14 us

profile of v3, /device:TPU:1, one launch (start us, length us, event | category | flops | bytes accessed | tf_op | source)
XLA Modules:
  0.0 40.6 jit_solution(3836191913703608561)
XLA Ops:
  0.6 36.8 %shard_map.103 = (f32[512,128]{1,0:T(8,128)}, f32[8,32,128]{2,1,0:T(8,128)}, f32[768,128]{1,0:T(8,128)}) custom-call(s32[8,8]{1,0:T(8,128)} %bitcast.18, s32[8]{0:T(128)} %bitcast.19, f32[32]{0:T(128)} %fcor_in.1, f32[768,128]{1,0:T(8,128)} %bitcast.13, f32[512,128]{1,0:T(8,128)} %bitcast.14, s32[128,128]{1,0:T(8,128)} %bitcast.15, s32[128,128]{1,0:T(8,128)} %bitcast.16, ...), custom_call_target="tpu_custom_call" | custom-call | flops 30000001024 | bytes 2000000 | tf_op jit(solution)/shard_map/pallas_call | solution.py:339
  37.5 0.0 copy-start.1
  37.5 0.0 copy-start
  37.5 1.7 %copy.14 = f32[1,1,128,4,128]{4,3,2,1,0:T(4,128)} copy(f32[1,1,128,4,128]{4,3,2,1,0:T(4,128)} %bitcast.11) | data formatting | bytes 524288
  39.2 0.0 copy-done.1
  39.2 0.7 %copy.15 = f32[1,1,8,8,4,128]{5,4,3,2,1,0:T(4,128)} copy(f32[1,1,8,8,4,128]{5,4,3,2,1,0:T(4,128)S(1)} %bitcast.12) | data formatting | bytes 262144
  39.9 0.0 copy-done
  39.9 0.7 %copy.16 = f32[2,12,32,128]{3,2,1,0:T(8,128)} copy(f32[2,12,32,128]{3,2,1,0:T(8,128)S(1)} %bitcast.10) | data formatting | bytes 786432
Async XLA Ops:
  37.5 1.7 %copy-start.1 = (f32[8,32,128]{2,1,0:T(8,128)S(1)}, f32[8,32,128]{2,1,0:T(8,128)}, u32[]{:S(2)}) copy-start(f32[8,32,128]{2,1,0:T(8,128)} %get-tuple-element.7) | copy-start | bytes 393220
  37.5 2.4 %copy-start = (f32[768,128]{1,0:T(8,128)S(1)}, f32[768,128]{1,0:T(8,128)}, u32[]{:S(2)}) copy-start(f32[768,128]{1,0:T(8,128)} %get-tuple-element.8) | copy-start | bytes 1179652

commit v4 on v3

--- a/solution.py
+++ b/solution.py
@@ -10,8 +10,8 @@
 MESH = pl.DeviceIdType.MESH
 LEV, CY, CX, NB = 12, 32, 128, 128
 ROWS = LEV * CY
-LOW = 128
-LAG = 4
+LAG = 8
+GREET = 3
 GRP = 8
 SPAN = GRP * 128
 STEPS = NB // GRP
@@ -116,23 +116,16 @@
         lon_out[half, 2:8, :] = jnp.zeros((6, ROWS), F32)
     lat_out[0] = winds[pl.ds(CY - 1, 2 * LEV, stride=CY), :]
     lat_out[1] = winds[pl.ds(0, 2 * LEV, stride=CY), :]
-    pl.semaphore_wait(barrier, 8)
     halos = [
         copy(lon_out.at[0], lon_in.at[0], 0, (0, 1)),
         copy(lon_out.at[1], lon_in.at[1], 1, (0, -1)),
         copy(lat_out.at[0], lat_in.at[0], 2, (1, 0)),
         copy(lat_out.at[1], lat_in.at[1], 3, (-1, 0)),
     ]
-    for each in halos:
-        each.start()
-
     def keep(field, flipped):
         high, low = split(flipped)
-        lines = slice(field * CX, (field + 1) * CX)
-        table[lines, 0:LOW] = high[:, :LOW]
-        table[lines, LOW : 2 * LOW] = low[:, :LOW]
-        table[lines, 2 * LOW : ROWS + LOW] = high[:, LOW:]
-        table[lines, ROWS + LOW : 2 * ROWS] = low[:, LOW:]
+        table[field * CX : (field + 1) * CX, 0:ROWS] = high
+        table[field * CX : (field + 1) * CX, ROWS : 2 * ROWS] = low
 
     for w in range(2):
         keep(w, level_diff(winds[w * ROWS : (w + 1) * ROWS, :]).T)
@@ -150,7 +143,6 @@
         across.append((north - south) * 0.5)
     words[0] = pack(*along)
     words[1] = pack(*across)
-    words[2] = pack(*[level_diff(winds[w * ROWS : (w + 1) * ROWS, :]) for w in range(2)])
     dep[...] = jnp.zeros((ROWS, 6 * CX), F32)
     for each in loads[1:]:
         each.wait()
@@ -166,18 +158,16 @@
         y = lax.shift_right_logical(cells, 7)
         return jnp.bitwise_and(cells, CX - 1), y, level[blocks_of(c), :] * CY + y
 
-    def rise(c, whole):
+    def rise(c, at):
         for i in range(GRP):
             cells = cell[pl.ds(c * GRP + i, 1), :]
             rows = level[pl.ds(c * GRP + i, 1), :] * CY + lax.shift_right_logical(cells, 7)
             hot = jnp.where(r_ids == rows, 1.0, 0.0).astype(BF16)
-            fresh[:, i * 128 : (i + 1) * 128] = hot
+            fresh[at, :, i * 128 : (i + 1) * 128] = hot
             hots[c, :, i * 128 : (i + 1) * 128] = hot
-        first, rest = fresh[:LOW, :], fresh[LOW:, :]
+        hot = fresh[at]
         picked = lax.dot_general(
-            table[...] if whole else table[:, 2 * LOW :],
-            jnp.concatenate([first, first, rest, rest] if whole else [rest, rest], axis=0),
-            (((1,), (0,)), ((), ())),
+            table[...], jnp.concatenate([hot, hot], axis=0), (((1,), (0,)), ((), ())),
             preferred_element_type=F32,
         )
         for i in range(GRP):
@@ -188,25 +178,23 @@
                     jnp.where(mask, part, 0.0), axis=0, keepdims=True
                 )
 
-    def pick(c, whole):
+    def pick(c):
         x, _, rows = place(c)
-        nought = jnp.full((GRP, 128), 32768, jnp.int32)
-        got = [nought] * 3
+        got = [jnp.zeros((GRP, 128), jnp.int32)] * 2
         for r in range(ROWS):
             here = rows == r
-            for w in range(2 if whole or r >= LOW else 3):
+            for w in range(2):
                 line = jnp.broadcast_to(words[w, r : r + 1, :], (GRP, CX))
                 taken = jnp.take_along_axis(line, x, axis=1, mode="promise_in_bounds")
                 got[w] = jnp.where(here, taken, got[w])
-        for w in range(3):
+        for w in range(2):
             found[w, blocks_of(c), :] = got[w]
 
     def advance(c):
         x, y, rows = place(c)
         levels = level[blocks_of(c), :]
         sample = [*unpack(found[0, blocks_of(c), :]), *unpack(found[1, blocks_of(c), :])]
-        for f, value in enumerate(unpack(found[2, blocks_of(c), :])):
-            sample.append(value + samples[f, blocks_of(c), :])
+        sample += [samples[0, blocks_of(c), :], samples[1, blocks_of(c), :]]
         lanes, tiles = jnp.bitwise_and(rows, 127), lax.shift_right_logical(rows, 7)
         nought = jnp.full((GRP, 128), 32768, jnp.int32)
         for side, end in ((0, 0), (1, CX - 1)):
@@ -259,8 +247,15 @@
         )
 
     def before(c, carry):
-        rise(c, True)
-        pick(c, True)
+        @pl.when(c == GREET)
+        def _():
+            pl.semaphore_wait(barrier, 8)
+            for each in halos:
+                each.start()
+
+        rise(2 * c, 0)
+        rise(2 * c + 1, 1)
+        pick(c)
         return carry
 
     lax.fori_loop(0, LAG, before, 0)
@@ -281,12 +276,17 @@
     def after(c, carry):
         scatter((0, 1, 2), c - LAG, [hots[c - LAG]])
         advance(c - LAG + 1)
-        pick(c, False)
-        rise(c, False)
+        pick(c)
         return carry
 
     lax.fori_loop(LAG, STEPS, after, 0)
-    lax.fori_loop(STEPS - LAG + 1, STEPS, lambda c, carry: (advance(c), carry)[1], 0)
+
+    def finish(c, carry):
+        scatter((2,), c, [hots[c]])
+        advance(c + 1)
+        return carry
+
+    lax.fori_loop(STEPS - LAG, STEPS - 1, finish, 0)
 
     boxes = []
     for d, where in enumerate(DIRS):
@@ -307,7 +307,7 @@
 
         lax.fori_loop(0, count // 2, step, 0)
 
-    last((2,), STEPS - LAG, LAG)
+    scatter((2,), STEPS - 1, [hots[STEPS - 1]])
     zonal = deposit(2).T
     wind_t[0] = zonal
     for half in range(2):
@@ -333,6 +333,19 @@
     arrived[...] = box_in[...]
 
 
+def deliver(*refs):
+    ins, outs, held, sem_in, sem_out = refs[:3], refs[3:6], refs[6:9], refs[9], refs[10]
+    loads = [pltpu.make_async_copy(ins[i], held[i], sem_in.at[i]) for i in range(3)]
+    stores = [pltpu.make_async_copy(held[i], outs[i], sem_out.at[i]) for i in range(3)]
+    for each in loads:
+        each.start()
+    for load, store in zip(loads, stores):
+        load.wait()
+        store.start()
+    for each in stores:
+        each.wait()
+
+
 def on_device(winds, coriolis, rays, ray_cell, ray_level, turning, leaving, leave_count):
     vmem = pl.BlockSpec(memory_space=pltpu.VMEM)
     hbm = pl.BlockSpec(memory_space=pltpu.HBM)
@@ -356,12 +369,12 @@
             pltpu.VMEM((NB, 128), jnp.int32),
             pltpu.VMEM((2, CX, ROWS), F32),
             pltpu.VMEM((2 * CX, 2 * ROWS), BF16),
-            pltpu.VMEM((3, ROWS, CX), jnp.int32),
+            pltpu.VMEM((2, ROWS, CX), jnp.int32),
             pltpu.VMEM((2, LEV, CX), jnp.int32),
             pltpu.VMEM((2, ROWS // 128, 128), jnp.int32),
-            pltpu.VMEM((ROWS, SPAN), BF16),
+            pltpu.VMEM((2, ROWS, SPAN), BF16),
             pltpu.VMEM((STEPS, ROWS, SPAN), BF16),
-            pltpu.VMEM((3, NB, 128), jnp.int32),
+            pltpu.VMEM((2, NB, 128), jnp.int32),
             pltpu.VMEM((2, NB, 128), F32),
             pltpu.VMEM((6, NB, 128), F32),
             pltpu.VMEM((ROWS, 6 * CX), F32),
@@ -391,6 +404,16 @@
         ray_level.reshape(NB, 128),
         turning.reshape(NB, 128),
     )
+    hbm = pl.BlockSpec(memory_space=pltpu.HBM)
+    rays_new, arrived, tendency = pl.pallas_call(
+        deliver,
+        out_shape=tuple(jax.ShapeDtypeStruct(each.shape, F32) for each in (rays_new, arrived, tendency)),
+        in_specs=[hbm] * 3,
+        out_specs=(hbm,) * 3,
+        scratch_shapes=[pltpu.VMEM(each.shape, F32) for each in (rays_new, arrived, tendency)]
+        + [pltpu.SemaphoreType.DMA((3,)), pltpu.SemaphoreType.DMA((3,))],
+        compiler_params=pltpu.CompilerParams(vmem_limit_bytes=62 << 20),
+    )(rays_new, arrived, tendency)
     return (
         rays_new.reshape(rays.shape),
         arrived.reshape(1, 1, 8, 8, 4, 128),

time: 41.4 us -> 37.9 us (0.915); the launches traced: 40.6 us -> 37.8 us
  local copies, waits for them, and re-layouts: 3.14 us -> 0 us
    unnamed x7 -> x0, local copies, waits for them, and re-layouts: 3.14 us -> none
    pallas_call x0 -> x1, Pallas kernels: none -> 1.94 us  [on_device(): pl.pallas_call(deliver, out_shape=tuple((jax.ShapeDtypeStruct(each.shape,...]
    pallas_call x1, Pallas kernels: 36.8 us -> 35.2 us  [on_device(): pl.pallas_call(kernel, out_shape=(jax.ShapeDtypeStruct((NB * 4, 128), F32...]
where the time goes in v4:
time: 37.9 us; the launch traced here: 37.8 us
  Pallas kernels  37.1 us (98%)
  between operations  0.64 us (2%)
    pallas_call x1, Pallas kernels, on_device(): pl.pallas_call(kernel, out_shape=(jax.ShapeDtypeStruct((NB * 4, 128), F32...  35.2 us
    pallas_call x1, Pallas kernels, on_device(): pl.pallas_call(deliver, out_shape=tuple((jax.ShapeDtypeStruct(each.shape,...  1.94 us

profile of v4, /device:TPU:1, one launch (start us, length us, event | category | flops | bytes accessed | tf_op | source)
XLA Modules:
  0.0 37.8 jit_solution(6386224744494118638)
XLA Ops:
  0.6 35.2 %shard_map.103 = (f32[512,128]{1,0:T(8,128)}, f32[8,32,128]{2,1,0:T(8,128)}, f32[768,128]{1,0:T(8,128)}) custom-call(s32[8,8]{1,0:T(8,128)} %bitcast.18, s32[8]{0:T(128)} %bitcast.19, f32[32]{0:T(128)} %fcor_in.1, f32[768,128]{1,0:T(8,128)} %bitcast.10, f32[512,128]{1,0:T(8,128)} %bitcast.12, s32[128,128]{1,0:T(8,128)} %bitcast.15, s32[128,128]{1,0:T(8,128)} %bitcast.16, ...), custom_call_target="tpu_custom_call" | custom-call | flops 30000001024 | bytes 2000000 | tf_op jit(solution)/shard_map/pallas_call | solution.py:352
  35.8 1.9 %shard_map.104 = (f32[512,128]{1,0:T(8,128)}, f32[8,32,128]{2,1,0:T(8,128)}, f32[768,128]{1,0:T(8,128)}) custom-call(f32[512,128]{1,0:T(8,128)} %get-tuple-element.9.refs_0_, f32[8,32,128]{2,1,0:T(8,128)} %get-tuple-element.10.refs_1_, f32[768,128]{1,0:T(8,128)} %get-tuple-element.11.refs_2_), custom_call_target="tpu_custom_call" | custom-call | tf_op jit(solution)/shard_map/pallas_call | solution.py:408

commit v5 on v4

--- a/solution.py
+++ b/solution.py
@@ -11,9 +11,10 @@
 LEV, CY, CX, NB = 12, 32, 128, 128
 ROWS = LEV * CY
 LAG = 8
-GREET = 3
+GREET = 4
 GRP = 8
 SPAN = GRP * 128
+HALF = SPAN // 2
 STEPS = NB // GRP
 UNIT = 5461.0
 F32, BF16 = jnp.float32, jnp.bfloat16
@@ -67,11 +68,11 @@
 
 def kernel(
     leaving_in, count_in, fcor_in, winds_in, rays_in, cell_in, level_in, turn_in,
-    rays_out, arrived, tend,
-    leaving, count, fcor, winds, rays, cell, level, turn,
+    rays_new, arrived, tendency,
+    rays_out, tend, leaving, count, fcor, winds, rays, cell, level, turn,
     wind_t, table, words, lat_edge, lon_edge, fresh, hots, found, samples, fluxes, dep,
-    lon_out, lon_in, lat_out, lat_in, edge_out, edge_in, box_out, box_in,
-    load_sem, send_sem, recv_sem,
+    lon_out, lon_in, lat_out, lat_in, edge_out, edge_in, box_out,
+    load_sem, store_sem, send_sem, recv_sem,
 ):
     loads = [
         pltpu.make_async_copy(src, dst, load_sem.at[i])
@@ -158,23 +159,25 @@
         y = lax.shift_right_logical(cells, 7)
         return jnp.bitwise_and(cells, CX - 1), y, level[blocks_of(c), :] * CY + y
 
-    def rise(c, at):
-        for i in range(GRP):
-            cells = cell[pl.ds(c * GRP + i, 1), :]
-            rows = level[pl.ds(c * GRP + i, 1), :] * CY + lax.shift_right_logical(cells, 7)
+    def rise(h, halves, at):
+        first = h * (GRP // 2)
+        for i in range(halves * GRP // 2):
+            cells = cell[pl.ds(first + i, 1), :]
+            rows = level[pl.ds(first + i, 1), :] * CY + lax.shift_right_logical(cells, 7)
             hot = jnp.where(r_ids == rows, 1.0, 0.0).astype(BF16)
             fresh[at, :, i * 128 : (i + 1) * 128] = hot
-            hots[c, :, i * 128 : (i + 1) * 128] = hot
-        hot = fresh[at]
+            lanes = slice(i % (GRP // 2) * 128, (i % (GRP // 2) + 1) * 128)
+            hots[h + i // (GRP // 2), :, lanes] = hot
+        hot = fresh[at, :, : halves * HALF]
         picked = lax.dot_general(
             table[...], jnp.concatenate([hot, hot], axis=0), (((1,), (0,)), ((), ())),
             preferred_element_type=F32,
         )
-        for i in range(GRP):
-            mask = x_ids == jnp.bitwise_and(cell[pl.ds(c * GRP + i, 1), :], CX - 1)
+        for i in range(halves * GRP // 2):
+            mask = x_ids == jnp.bitwise_and(cell[pl.ds(first + i, 1), :], CX - 1)
             for f in range(2):
                 part = picked[f * CX : (f + 1) * CX, i * 128 : (i + 1) * 128]
-                samples[f, pl.ds(c * GRP + i, 1), :] = jnp.sum(
+                samples[f, pl.ds(first + i, 1), :] = jnp.sum(
                     jnp.where(mask, part, 0.0), axis=0, keepdims=True
                 )
 
@@ -225,15 +228,18 @@
             fluxes[2 * j, blocks_of(c), :] = high
             fluxes[2 * j + 1, blocks_of(c), :] = out[3 + j] - high
 
-    def scatter(js, c, hot):
+    def hot_of(c, steps):
+        return [hots[2 * c + i] for i in range(2 * steps)]
+
+    def scatter(js, c, hot, source=None):
+        source = c if source is None else source
         parts = []
-        for i in range(len(hot) * GRP):
-            at_row = pl.ds(c * GRP + i, 1)
-            mask = x_ids == jnp.bitwise_and(cell[at_row, :], CX - 1)
+        for i in range(len(hot) * GRP // 2):
+            mask = x_ids == jnp.bitwise_and(cell[pl.ds(c * GRP + i, 1), :], CX - 1)
             parts.append(
                 jnp.concatenate(
                     [
-                        jnp.where(mask, fluxes[2 * j + p, at_row, :], 0.0).astype(BF16)
+                        jnp.where(mask, fluxes[2 * j + p, pl.ds(source * GRP + i, 1), :], 0.0).astype(BF16)
                         for j in js
                         for p in range(2)
                     ],
@@ -253,8 +259,8 @@
             for each in halos:
                 each.start()
 
-        rise(2 * c, 0)
-        rise(2 * c + 1, 1)
+        rise(2 * c, 2, 0)
+        rise(2 * LAG + c, 1, 1)
         pick(c)
         return carry
 
@@ -272,28 +278,28 @@
             *[jnp.where(closed, 0.0, lat_in[side, w * LEV : (w + 1) * LEV, :] * sign) for w in range(2)]
         )
     advance(0)
-
-    def after(c, carry):
-        scatter((0, 1, 2), c - LAG, [hots[c - LAG]])
-        advance(c - LAG + 1)
-        pick(c)
+    advance(1)
+    fluxes[:, NB : NB + 2 * GRP, :] = jnp.zeros((6, 2 * GRP, 128), F32)
+
+    def after(i, carry):
+        pair = jnp.maximum(2 * i - 2, 0)
+        source = jnp.where(i == 0, STEPS, 2 * i - 2)
+        scatter((2,), pair, hot_of(pair, 2), source)
+        advance(jnp.minimum(2 * i + 2, LAG - 2 + i))
+        advance(jnp.minimum(2 * i + 3, LAG - 1 + i))
+        rise(3 * LAG + i, 1, 0)
+        pick(LAG + i)
         return carry
 
-    lax.fori_loop(LAG, STEPS, after, 0)
-
-    def finish(c, carry):
-        scatter((2,), c, [hots[c]])
-        advance(c + 1)
-        return carry
-
-    lax.fori_loop(STEPS - LAG, STEPS - 1, finish, 0)
+    lax.fori_loop(0, STEPS - LAG, after, 0)
+    advance(STEPS - 1)
 
     boxes = []
     for d, where in enumerate(DIRS):
         for slot in range(8):
             block = rays_out[pl.ds(leaving[d, slot] * 4, 4), :]
             box_out[d, slot * 4 : slot * 4 + 4, :] = jnp.where(slot < count[d], block, 0.0)
-        boxes.append(copy(box_out.at[d], box_in.at[d], 4 + d, where))
+        boxes.append(copy(box_out.at[d], arrived.at[d], 4 + d, where))
         boxes[-1].start()
 
     def deposit(j):
@@ -302,14 +308,15 @@
 
     def last(js, first, count):
         def step(c, carry):
-            scatter(js, first + 2 * c, [hots[first + 2 * c], hots[first + 2 * c + 1]])
+            scatter(js, first + 2 * c, hot_of(first + 2 * c, 2))
             return carry
 
         lax.fori_loop(0, count // 2, step, 0)
 
-    scatter((2,), STEPS - 1, [hots[STEPS - 1]])
+    stores = [pltpu.make_async_copy(rays_out, rays_new, store_sem.at[0])]
+    stores[0].start()
+    last((2,), STEPS - 2, 2)
     zonal = deposit(2).T
-    wind_t[0] = zonal
     for half in range(2):
         edge_out[half] = jnp.zeros((8, ROWS), F32)
     edge_out[0, 0:1, :] = zonal[CX - 1 : CX, :]
@@ -320,17 +327,24 @@
     ]
     for each in edges:
         each.start()
-    last((0, 1), STEPS - LAG, LAG)
+    last((0, 1), 0, STEPS)
     tend[ROWS : 2 * ROWS, :] = -level_diff(deposit(1))
+    half = pl.ds(ROWS, ROWS)
+    stores.append(pltpu.make_async_copy(tend.at[half], tendency.at[half], store_sem.at[1]))
+    stores[1].start()
+    zonal = deposit(2)
+    east = jnp.where(lane == CX - 1, 0.0, pltpu.roll(zonal, CX - 1, 1))
+    west = jnp.where(lane == 0, 0.0, pltpu.roll(zonal, 1, 1))
+    tend[0:ROWS, :] = -level_diff(deposit(0)) - (east - west) * 0.5
     for each in edges:
         each.wait()
-    zonal = wind_t[0]
-    east = jnp.where(column == CX - 1, edge_in[1, 0:1, :], pltpu.roll(zonal, CX - 1, 0))
-    west = jnp.where(column == 0, edge_in[0, 0:1, :], pltpu.roll(zonal, 1, 0))
-    tend[0:ROWS, :] = -level_diff(deposit(0)) - ((east - west) * 0.5).T
-    for each in boxes:
+    beyond = jnp.where(column == CX - 1, edge_in[1, 0:1, :] * -0.5, 0.0)
+    tend[0:ROWS, :] += jnp.where(column == 0, edge_in[0, 0:1, :] * 0.5, beyond).T
+    half = pl.ds(0, ROWS)
+    stores.append(pltpu.make_async_copy(tend.at[half], tendency.at[half], store_sem.at[2]))
+    stores[2].start()
+    for each in (*boxes, *stores):
         each.wait()
-    arrived[...] = box_in[...]
 
 
 def deliver(*refs):
@@ -347,7 +361,6 @@
 
 
 def on_device(winds, coriolis, rays, ray_cell, ray_level, turning, leaving, leave_count):
-    vmem = pl.BlockSpec(memory_space=pltpu.VMEM)
     hbm = pl.BlockSpec(memory_space=pltpu.HBM)
     rays_new, arrived, tendency = pl.pallas_call(
         kernel,
@@ -357,8 +370,10 @@
             jax.ShapeDtypeStruct((2 * ROWS, CX), F32),
         ),
         in_specs=[hbm] * 8,
-        out_specs=(vmem, vmem, vmem),
+        out_specs=(hbm,) * 3,
         scratch_shapes=[
+            pltpu.VMEM((NB * 4, 128), F32),
+            pltpu.VMEM((2 * ROWS, CX), F32),
             pltpu.SMEM((8, 8), jnp.int32),
             pltpu.SMEM((8,), jnp.int32),
             pltpu.SMEM((32,), F32),
@@ -373,10 +388,10 @@
             pltpu.VMEM((2, LEV, CX), jnp.int32),
             pltpu.VMEM((2, ROWS // 128, 128), jnp.int32),
             pltpu.VMEM((2, ROWS, SPAN), BF16),
-            pltpu.VMEM((STEPS, ROWS, SPAN), BF16),
+            pltpu.VMEM((2 * STEPS, ROWS, HALF), BF16),
             pltpu.VMEM((2, NB, 128), jnp.int32),
             pltpu.VMEM((2, NB, 128), F32),
-            pltpu.VMEM((6, NB, 128), F32),
+            pltpu.VMEM((6, NB + 2 * GRP, 128), F32),
             pltpu.VMEM((ROWS, 6 * CX), F32),
             pltpu.VMEM((2, 8, ROWS), F32),
             pltpu.VMEM((2, 8, ROWS), F32),
@@ -385,8 +400,8 @@
             pltpu.VMEM((2, 8, ROWS), F32),
             pltpu.VMEM((2, 8, ROWS), F32),
             pltpu.VMEM((8, 32, 128), F32),
-            pltpu.VMEM((8, 32, 128), F32),
             pltpu.SemaphoreType.DMA((8,)),
+            pltpu.SemaphoreType.DMA((3,)),
             pltpu.SemaphoreType.DMA((14,)),
             pltpu.SemaphoreType.DMA((14,)),
         ],
@@ -404,7 +419,6 @@
         ray_level.reshape(NB, 128),
         turning.reshape(NB, 128),
     )
-    hbm = pl.BlockSpec(memory_space=pltpu.HBM)
     rays_new, arrived, tendency = pl.pallas_call(
         deliver,
         out_shape=tuple(jax.ShapeDtypeStruct(each.shape, F32) for each in (rays_new, arrived, tendency)),

time: 37.9 us -> 36.9 us (0.974)
  Pallas kernels: 37.1 us -> 36 us
    pallas_call x1, Pallas kernels: 35.2 us -> 34.1 us  [on_device(): pl.pallas_call(kernel, out_shape=(jax.ShapeDtypeStruct((NB * 4, 128), F32...]
where the time goes in v5:
time: 36.9 us; the launch traced here: 36.6 us
  Pallas kernels  36 us (98%)
  between operations  0.64 us (2%)
    pallas_call x1, Pallas kernels, on_device(): pl.pallas_call(kernel, out_shape=(jax.ShapeDtypeStruct((NB * 4, 128), F32...  34.1 us
    pallas_call x1, Pallas kernels, on_device(): pl.pallas_call(deliver, out_shape=tuple((jax.ShapeDtypeStruct(each.shape,...  1.94 us

profile of v5, /device:TPU:1, one launch (start us, length us, event | category | flops | bytes accessed | tf_op | source)
XLA Modules:
  0.0 36.6 jit_solution(13631044389244834598)
XLA Ops:
  0.6 34.1 %shard_map.103 = (f32[512,128]{1,0:T(8,128)}, f32[8,32,128]{2,1,0:T(8,128)}, f32[768,128]{1,0:T(8,128)}) custom-call(s32[8,8]{1,0:T(8,128)} %bitcast.18, s32[8]{0:T(128)} %bitcast.19, f32[32]{0:T(128)} %fcor_in.1, f32[768,128]{1,0:T(8,128)} %bitcast.10, f32[512,128]{1,0:T(8,128)} %bitcast.12, s32[128,128]{1,0:T(8,128)} %bitcast.15, s32[128,128]{1,0:T(8,128)} %bitcast.16, ...), custom_call_target="tpu_custom_call" | custom-call | flops 30000001024 | bytes 2000000 | tf_op jit(solution)/shard_map/pallas_call | solution.py:365
  34.7 1.9 %shard_map.104 = (f32[512,128]{1,0:T(8,128)}, f32[8,32,128]{2,1,0:T(8,128)}, f32[768,128]{1,0:T(8,128)}) custom-call(f32[512,128]{1,0:T(8,128)} %get-tuple-element.9.refs_0_, f32[8,32,128]{2,1,0:T(8,128)} %get-tuple-element.10.refs_1_, f32[768,128]{1,0:T(8,128)} %get-tuple-element.11.refs_2_), custom_call_target="tpu_custom_call" | custom-call | tf_op jit(solution)/shard_map/pallas_call | solution.py:422

commit v6 on v5

--- a/solution.py
+++ b/solution.py
@@ -11,7 +11,7 @@
 LEV, CY, CX, NB = 12, 32, 128, 128
 ROWS = LEV * CY
 LAG = 8
-GREET = 4
+GREET = 2
 GRP = 8
 SPAN = GRP * 128
 HALF = SPAN // 2
@@ -107,14 +107,17 @@
     for where in DIRS:
         pl.semaphore_signal(barrier, inc=1, device_id=at(*where), device_id_type=MESH)
 
+    dep[...] = jnp.zeros((ROWS, 6 * CX), F32)
+    fluxes[:, NB : NB + 2 * GRP, :] = jnp.zeros((6, 2 * GRP, 128), F32)
+    for half in range(2):
+        lon_out[half, 2:8, :] = jnp.zeros((6, ROWS), F32)
+        edge_out[half] = jnp.zeros((8, ROWS), F32)
     loads[0].wait()
     for w in range(2):
         flipped = winds[w * ROWS : (w + 1) * ROWS, :].T
         wind_t[w] = flipped
         lon_out[0, w : w + 1, :] = flipped[CX - 1 : CX, :]
         lon_out[1, w : w + 1, :] = flipped[0:1, :]
-    for half in range(2):
-        lon_out[half, 2:8, :] = jnp.zeros((6, ROWS), F32)
     lat_out[0] = winds[pl.ds(CY - 1, 2 * LEV, stride=CY), :]
     lat_out[1] = winds[pl.ds(0, 2 * LEV, stride=CY), :]
     halos = [
@@ -144,7 +147,6 @@
         across.append((north - south) * 0.5)
     words[0] = pack(*along)
     words[1] = pack(*across)
-    dep[...] = jnp.zeros((ROWS, 6 * CX), F32)
     for each in loads[1:]:
         each.wait()
 
@@ -279,7 +281,6 @@
         )
     advance(0)
     advance(1)
-    fluxes[:, NB : NB + 2 * GRP, :] = jnp.zeros((6, 2 * GRP, 128), F32)
 
     def after(i, carry):
         pair = jnp.maximum(2 * i - 2, 0)
@@ -317,8 +318,6 @@
     stores[0].start()
     last((2,), STEPS - 2, 2)
     zonal = deposit(2).T
-    for half in range(2):
-        edge_out[half] = jnp.zeros((8, ROWS), F32)
     edge_out[0, 0:1, :] = zonal[CX - 1 : CX, :]
     edge_out[1, 0:1, :] = zonal[0:1, :]
     edges = [

time: 36.9 us -> 38.1 us (1.033)
  Pallas kernels: 36 us -> 37.3 us
    pallas_call x1, Pallas kernels: 34.1 us -> 35.4 us  [on_device(): pl.pallas_call(kernel, out_shape=(jax.ShapeDtypeStruct((NB * 4, 128), F32...]
where the time goes in v6:
time: 38.1 us; the launch traced here: 38 us
  Pallas kernels  37.3 us (98%)
  between operations  0.64 us (2%)
    pallas_call x1, Pallas kernels, on_device(): pl.pallas_call(kernel, out_shape=(jax.ShapeDtypeStruct((NB * 4, 128), F32...  35.4 us
    pallas_call x1, Pallas kernels, on_device(): pl.pallas_call(deliver, out_shape=tuple((jax.ShapeDtypeStruct(each.shape,...  1.94 us

profile of v6, /device:TPU:1, one launch (start us, length us, event | category | flops | bytes accessed | tf_op | source)
XLA Modules:
  0.0 38.0 jit_solution(14424818975884012273)
XLA Ops:
  0.6 35.4 %shard_map.103 = (f32[512,128]{1,0:T(8,128)}, f32[8,32,128]{2,1,0:T(8,128)}, f32[768,128]{1,0:T(8,128)}) custom-call(s32[8,8]{1,0:T(8,128)} %bitcast.18, s32[8]{0:T(128)} %bitcast.19, f32[32]{0:T(128)} %fcor_in.1, f32[768,128]{1,0:T(8,128)} %bitcast.10, f32[512,128]{1,0:T(8,128)} %bitcast.12, s32[128,128]{1,0:T(8,128)} %bitcast.15, s32[128,128]{1,0:T(8,128)} %bitcast.16, ...), custom_call_target="tpu_custom_call" | custom-call | flops 30000001024 | bytes 2000000 | tf_op jit(solution)/shard_map/pallas_call | solution.py:364
  36.0 1.9 %shard_map.104 = (f32[512,128]{1,0:T(8,128)}, f32[8,32,128]{2,1,0:T(8,128)}, f32[768,128]{1,0:T(8,128)}) custom-call(f32[512,128]{1,0:T(8,128)} %get-tuple-element.9.refs_0_, f32[8,32,128]{2,1,0:T(8,128)} %get-tuple-element.10.refs_1_, f32[768,128]{1,0:T(8,128)} %get-tuple-element.11.refs_2_), custom_call_target="tpu_custom_call" | custom-call | tf_op jit(solution)/shard_map/pallas_call | solution.py:421

commit v7 on v6

--- a/solution.py
+++ b/solution.py
@@ -11,7 +11,7 @@
 LEV, CY, CX, NB = 12, 32, 128, 128
 ROWS = LEV * CY
 LAG = 8
-GREET = 2
+GREET = 4
 GRP = 8
 SPAN = GRP * 128
 HALF = SPAN // 2
@@ -74,6 +74,22 @@
     lon_out, lon_in, lat_out, lat_in, edge_out, edge_in, box_out,
     load_sem, store_sem, send_sem, recv_sem,
 ):
+    lon, lat = lax.axis_index("lon"), lax.axis_index("lat")
+    nlon, nlat = lax.axis_size("lon"), lax.axis_size("lat")
+
+    def at(dlat, dlon):
+        return (lax.rem(lon + dlon + nlon, nlon), lax.rem(lat + dlat + nlat, nlat))
+
+    def copy(src, dst, which, where):
+        return pltpu.make_async_remote_copy(
+            src_ref=src, dst_ref=dst, send_sem=send_sem.at[which], recv_sem=recv_sem.at[which],
+            device_id=at(*where), device_id_type=MESH,
+        )
+
+    barrier = pltpu.get_barrier_semaphore()
+    for where in DIRS:
+        pl.semaphore_signal(barrier, inc=1, device_id=at(*where), device_id_type=MESH)
+
     loads = [
         pltpu.make_async_copy(src, dst, load_sem.at[i])
         for i, (src, dst) in enumerate(
@@ -91,27 +107,8 @@
     ]
     for each in loads:
         each.start()
-    lon, lat = lax.axis_index("lon"), lax.axis_index("lat")
-    nlon, nlat = lax.axis_size("lon"), lax.axis_size("lat")
-
-    def at(dlat, dlon):
-        return (lax.rem(lon + dlon + nlon, nlon), lax.rem(lat + dlat + nlat, nlat))
-
-    def copy(src, dst, which, where):
-        return pltpu.make_async_remote_copy(
-            src_ref=src, dst_ref=dst, send_sem=send_sem.at[which], recv_sem=recv_sem.at[which],
-            device_id=at(*where), device_id_type=MESH,
-        )
-
-    barrier = pltpu.get_barrier_semaphore()
-    for where in DIRS:
-        pl.semaphore_signal(barrier, inc=1, device_id=at(*where), device_id_type=MESH)
-
     dep[...] = jnp.zeros((ROWS, 6 * CX), F32)
     fluxes[:, NB : NB + 2 * GRP, :] = jnp.zeros((6, 2 * GRP, 128), F32)
-    for half in range(2):
-        lon_out[half, 2:8, :] = jnp.zeros((6, ROWS), F32)
-        edge_out[half] = jnp.zeros((8, ROWS), F32)
     loads[0].wait()
     for w in range(2):
         flipped = winds[w * ROWS : (w + 1) * ROWS, :].T
@@ -161,25 +158,25 @@
         y = lax.shift_right_logical(cells, 7)
         return jnp.bitwise_and(cells, CX - 1), y, level[blocks_of(c), :] * CY + y
 
-    def rise(h, halves, at):
-        first = h * (GRP // 2)
-        for i in range(halves * GRP // 2):
-            cells = cell[pl.ds(first + i, 1), :]
-            rows = level[pl.ds(first + i, 1), :] * CY + lax.shift_right_logical(cells, 7)
+    def rise(halves):
+        blocks = [h * (GRP // 2) + i for h in halves for i in range(GRP // 2)]
+        for i, block in enumerate(blocks):
+            cells = cell[pl.ds(block, 1), :]
+            rows = level[pl.ds(block, 1), :] * CY + lax.shift_right_logical(cells, 7)
             hot = jnp.where(r_ids == rows, 1.0, 0.0).astype(BF16)
-            fresh[at, :, i * 128 : (i + 1) * 128] = hot
+            fresh[:, i * 128 : (i + 1) * 128] = hot
             lanes = slice(i % (GRP // 2) * 128, (i % (GRP // 2) + 1) * 128)
-            hots[h + i // (GRP // 2), :, lanes] = hot
-        hot = fresh[at, :, : halves * HALF]
+            hots[halves[i // (GRP // 2)], :, lanes] = hot
+        hot = fresh[:, : len(halves) * HALF]
         picked = lax.dot_general(
             table[...], jnp.concatenate([hot, hot], axis=0), (((1,), (0,)), ((), ())),
             preferred_element_type=F32,
         )
-        for i in range(halves * GRP // 2):
-            mask = x_ids == jnp.bitwise_and(cell[pl.ds(first + i, 1), :], CX - 1)
+        for i, block in enumerate(blocks):
+            mask = x_ids == jnp.bitwise_and(cell[pl.ds(block, 1), :], CX - 1)
             for f in range(2):
                 part = picked[f * CX : (f + 1) * CX, i * 128 : (i + 1) * 128]
-                samples[f, pl.ds(first + i, 1), :] = jnp.sum(
+                samples[f, pl.ds(block, 1), :] = jnp.sum(
                     jnp.where(mask, part, 0.0), axis=0, keepdims=True
                 )
 
@@ -261,8 +258,7 @@
             for each in halos:
                 each.start()
 
-        rise(2 * c, 2, 0)
-        rise(2 * LAG + c, 1, 1)
+        rise((2 * c, 2 * c + 1, 2 * LAG + c))
         pick(c)
         return carry
 
@@ -288,7 +284,7 @@
         scatter((2,), pair, hot_of(pair, 2), source)
         advance(jnp.minimum(2 * i + 2, LAG - 2 + i))
         advance(jnp.minimum(2 * i + 3, LAG - 1 + i))
-        rise(3 * LAG + i, 1, 0)
+        rise((3 * LAG + i,))
         pick(LAG + i)
         return carry
 
@@ -386,18 +382,18 @@
             pltpu.VMEM((2, ROWS, CX), jnp.int32),
             pltpu.VMEM((2, LEV, CX), jnp.int32),
             pltpu.VMEM((2, ROWS // 128, 128), jnp.int32),
-            pltpu.VMEM((2, ROWS, SPAN), BF16),
+            pltpu.VMEM((ROWS, 3 * HALF), BF16),
             pltpu.VMEM((2 * STEPS, ROWS, HALF), BF16),
             pltpu.VMEM((2, NB, 128), jnp.int32),
             pltpu.VMEM((2, NB, 128), F32),
             pltpu.VMEM((6, NB + 2 * GRP, 128), F32),
             pltpu.VMEM((ROWS, 6 * CX), F32),
-            pltpu.VMEM((2, 8, ROWS), F32),
-            pltpu.VMEM((2, 8, ROWS), F32),
+            pltpu.VMEM((2, 2, ROWS), F32),
+            pltpu.VMEM((2, 2, ROWS), F32),
             pltpu.VMEM((2, 2 * LEV, CX), F32),
             pltpu.VMEM((2, 2 * LEV, CX), F32),
-            pltpu.VMEM((2, 8, ROWS), F32),
-            pltpu.VMEM((2, 8, ROWS), F32),
+            pltpu.VMEM((2, 1, ROWS), F32),
+            pltpu.VMEM((2, 1, ROWS), F32),
             pltpu.VMEM((8, 32, 128), F32),
             pltpu.SemaphoreType.DMA((8,)),
             pltpu.SemaphoreType.DMA((3,)),

time: 38.1 us -> 36.6 us (0.961)
  Pallas kernels: 37.3 us -> 35.7 us
    pallas_call x1, Pallas kernels: 35.4 us -> 33.7 us  [on_device(): pl.pallas_call(kernel, out_shape=(jax.ShapeDtypeStruct((NB * 4, 128), F32...]
where the time goes in v7:
time: 36.6 us; the launch traced here: 36.3 us
  Pallas kernels  35.7 us (98%)
  between operations  0.64 us (2%)
    pallas_call x1, Pallas kernels, on_device(): pl.pallas_call(kernel, out_shape=(jax.ShapeDtypeStruct((NB * 4, 128), F32...  33.7 us
    pallas_call x1, Pallas kernels, on_device(): pl.pallas_call(deliver, out_shape=tuple((jax.ShapeDtypeStruct(each.shape,...  1.94 us

profile of v7, /device:TPU:1, one launch (start us, length us, event | category | flops | bytes accessed | tf_op | source)
XLA Modules:
  0.0 36.3 jit_solution(13062498690460483183)
XLA Ops:
  0.6 33.7 %shard_map.103 = (f32[512,128]{1,0:T(8,128)}, f32[8,32,128]{2,1,0:T(8,128)}, f32[768,128]{1,0:T(8,128)}) custom-call(s32[8,8]{1,0:T(8,128)} %bitcast.18, s32[8]{0:T(128)} %bitcast.19, f32[32]{0:T(128)} %fcor_in.1, f32[768,128]{1,0:T(8,128)} %bitcast.10, f32[512,128]{1,0:T(8,128)} %bitcast.12, s32[128,128]{1,0:T(8,128)} %bitcast.15, s32[128,128]{1,0:T(8,128)} %bitcast.16, ...), custom_call_target="tpu_custom_call" | custom-call | flops 30000001024 | bytes 2000000 | tf_op jit(solution)/shard_map/pallas_call | solution.py:360
  34.4 1.9 %shard_map.104 = (f32[512,128]{1,0:T(8,128)}, f32[8,32,128]{2,1,0:T(8,128)}, f32[768,128]{1,0:T(8,128)}) custom-call(f32[512,128]{1,0:T(8,128)} %get-tuple-element.9.refs_0_, f32[8,32,128]{2,1,0:T(8,128)} %get-tuple-element.10.refs_1_, f32[768,128]{1,0:T(8,128)} %get-tuple-element.11.refs_2_), custom_call_target="tpu_custom_call" | custom-call | tf_op jit(solution)/shard_map/pallas_call | solution.py:417

commit v8 on v7

--- a/solution.py
+++ b/solution.py
@@ -11,7 +11,7 @@
 LEV, CY, CX, NB = 12, 32, 128, 128
 ROWS = LEV * CY
 LAG = 8
-GREET = 4
+GREET = 2
 GRP = 8
 SPAN = GRP * 128
 HALF = SPAN // 2
@@ -251,8 +251,10 @@
             preferred_element_type=F32,
         )
 
+    greet = jnp.where(lax.rem(lon, 4) == 0, GREET + 2, GREET)
+
     def before(c, carry):
-        @pl.when(c == GREET)
+        @pl.when(c == greet)
         def _():
             pl.semaphore_wait(barrier, 8)
             for each in halos:
@@ -303,12 +305,12 @@
         return dep[:, j * 2 * CX : j * 2 * CX + CX] + dep[:, j * 2 * CX + CX : (j + 1) * 2 * CX]
 
 
-    def last(js, first, count):
+    def last(js, first, count, each=2):
         def step(c, carry):
-            scatter(js, first + 2 * c, hot_of(first + 2 * c, 2))
+            scatter(js, first + each * c, hot_of(first + each * c, each))
             return carry
 
-        lax.fori_loop(0, count // 2, step, 0)
+        lax.fori_loop(0, count // each, step, 0)
 
     stores = [pltpu.make_async_copy(rays_out, rays_new, store_sem.at[0])]
     stores[0].start()
@@ -322,7 +324,7 @@
     ]
     for each in edges:
         each.start()
-    last((0, 1), 0, STEPS)
+    last((0, 1), 0, STEPS, 4)
     tend[ROWS : 2 * ROWS, :] = -level_diff(deposit(1))
     half = pl.ds(ROWS, ROWS)
     stores.append(pltpu.make_async_copy(tend.at[half], tendency.at[half], store_sem.at[1]))

time: 36.6 us -> 34.7 us (0.948)
  Pallas kernels: 35.7 us -> 33.9 us
    pallas_call x1, Pallas kernels: 33.7 us -> 32 us  [on_device(): pl.pallas_call(kernel, out_shape=(jax.ShapeDtypeStruct((NB * 4, 128), F32...]
where the time goes in v8:
time: 34.7 us; the launch traced here: 34.6 us
  Pallas kernels  33.9 us (98%)
  between operations  0.64 us (2%)
    pallas_call x1, Pallas kernels, on_device(): pl.pallas_call(kernel, out_shape=(jax.ShapeDtypeStruct((NB * 4, 128), F32...  32 us
    pallas_call x1, Pallas kernels, on_device(): pl.pallas_call(deliver, out_shape=tuple((jax.ShapeDtypeStruct(each.shape,...  1.94 us

profile of v8, /device:TPU:1, one launch (start us, length us, event | category | flops | bytes accessed | tf_op | source)
XLA Modules:
  0.0 34.6 jit_solution(11514962851886866407)
XLA Ops:
  0.6 32.0 %shard_map.103 = (f32[512,128]{1,0:T(8,128)}, f32[8,32,128]{2,1,0:T(8,128)}, f32[768,128]{1,0:T(8,128)}) custom-call(s32[8,8]{1,0:T(8,128)} %bitcast.18, s32[8]{0:T(128)} %bitcast.19, f32[32]{0:T(128)} %fcor_in.1, f32[768,128]{1,0:T(8,128)} %bitcast.10, f32[512,128]{1,0:T(8,128)} %bitcast.12, s32[128,128]{1,0:T(8,128)} %bitcast.15, s32[128,128]{1,0:T(8,128)} %bitcast.16, ...), custom_call_target="tpu_custom_call" | custom-call | flops 30000001024 | bytes 2000000 | tf_op jit(solution)/shard_map/pallas_call | solution.py:362
  32.6 1.9 %shard_map.104 = (f32[512,128]{1,0:T(8,128)}, f32[8,32,128]{2,1,0:T(8,128)}, f32[768,128]{1,0:T(8,128)}) custom-call(f32[512,128]{1,0:T(8,128)} %get-tuple-element.9.refs_0_, f32[8,32,128]{2,1,0:T(8,128)} %get-tuple-element.10.refs_1_, f32[768,128]{1,0:T(8,128)} %get-tuple-element.11.refs_2_), custom_call_target="tpu_custom_call" | custom-call | tf_op jit(solution)/shard_map/pallas_call | solution.py:419

commit v9 on v8

--- a/solution.py
+++ b/solution.py
@@ -251,7 +251,7 @@
             preferred_element_type=F32,
         )
 
-    greet = jnp.where(lax.rem(lon, 4) == 0, GREET + 2, GREET)
+    greet = jnp.where(lon == 0, GREET + 3, jnp.where(lax.rem(lon, 4) == 0, GREET + 2, GREET))
 
     def before(c, carry):
         @pl.when(c == greet)

time: 34.7 us -> 33.9 us (0.977)
  Pallas kernels: 33.9 us -> 33.2 us
    pallas_call x1, Pallas kernels: 32 us -> 31.2 us  [on_device(): pl.pallas_call(kernel, out_shape=(jax.ShapeDtypeStruct((NB * 4, 128), F32...]
where the time goes in v9:
time: 33.9 us; the launch traced here: 33.8 us
  Pallas kernels  33.2 us (98%)
  between operations  0.64 us (2%)
    pallas_call x1, Pallas kernels, on_device(): pl.pallas_call(kernel, out_shape=(jax.ShapeDtypeStruct((NB * 4, 128), F32...  31.2 us
    pallas_call x1, Pallas kernels, on_device(): pl.pallas_call(deliver, out_shape=tuple((jax.ShapeDtypeStruct(each.shape,...  1.94 us

profile of v9, /device:TPU:1, one launch (start us, length us, event | category | flops | bytes accessed | tf_op | source)
XLA Modules:
  0.0 33.8 jit_solution(4500085088791436383)
XLA Ops:
  0.6 31.2 %shard_map.103 = (f32[512,128]{1,0:T(8,128)}, f32[8,32,128]{2,1,0:T(8,128)}, f32[768,128]{1,0:T(8,128)}) custom-call(s32[8,8]{1,0:T(8,128)} %bitcast.18, s32[8]{0:T(128)} %bitcast.19, f32[32]{0:T(128)} %fcor_in.1, f32[768,128]{1,0:T(8,128)} %bitcast.10, f32[512,128]{1,0:T(8,128)} %bitcast.12, s32[128,128]{1,0:T(8,128)} %bitcast.15, s32[128,128]{1,0:T(8,128)} %bitcast.16, ...), custom_call_target="tpu_custom_call" | custom-call | flops 30000001024 | bytes 2000000 | tf_op jit(solution)/shard_map/pallas_call | solution.py:362
  31.9 1.9 %shard_map.104 = (f32[512,128]{1,0:T(8,128)}, f32[8,32,128]{2,1,0:T(8,128)}, f32[768,128]{1,0:T(8,128)}) custom-call(f32[512,128]{1,0:T(8,128)} %get-tuple-element.9.refs_0_, f32[8,32,128]{2,1,0:T(8,128)} %get-tuple-element.10.refs_1_, f32[768,128]{1,0:T(8,128)} %get-tuple-element.11.refs_2_), custom_call_target="tpu_custom_call" | custom-call | tf_op jit(solution)/shard_map/pallas_call | solution.py:419

commit v10 on v9

--- a/solution.py
+++ b/solution.py
@@ -284,6 +284,7 @@
         pair = jnp.maximum(2 * i - 2, 0)
         source = jnp.where(i == 0, STEPS, 2 * i - 2)
         scatter((2,), pair, hot_of(pair, 2), source)
+        scatter((1,), i, hot_of(i, 1))
         advance(jnp.minimum(2 * i + 2, LAG - 2 + i))
         advance(jnp.minimum(2 * i + 3, LAG - 1 + i))
         rise((3 * LAG + i,))
@@ -324,7 +325,8 @@
     ]
     for each in edges:
         each.start()
-    last((0, 1), 0, STEPS, 4)
+    last((0, 1), LAG, STEPS - LAG, 8)
+    last((0,), 0, LAG, 8)
     tend[ROWS : 2 * ROWS, :] = -level_diff(deposit(1))
     half = pl.ds(ROWS, ROWS)
     stores.append(pltpu.make_async_copy(tend.at[half], tendency.at[half], store_sem.at[1]))

time: 33.9 us -> 34.9 us (1.029)
  Pallas kernels: 33.2 us -> 34.1 us
    pallas_call x1, Pallas kernels: 31.2 us -> 32.1 us  [on_device(): pl.pallas_call(kernel, out_shape=(jax.ShapeDtypeStruct((NB * 4, 128), F32...]
where the time goes in v10:
time: 34.9 us; the launch traced here: 34.7 us
  Pallas kernels  34.1 us (98%)
  between operations  0.64 us (2%)
    pallas_call x1, Pallas kernels, on_device(): pl.pallas_call(kernel, out_shape=(jax.ShapeDtypeStruct((NB * 4, 128), F32...  32.1 us
    pallas_call x1, Pallas kernels, on_device(): pl.pallas_call(deliver, out_shape=tuple((jax.ShapeDtypeStruct(each.shape,...  1.94 us

profile of v10, /device:TPU:1, one launch (start us, length us, event | category | flops | bytes accessed | tf_op | source)
XLA Modules:
  0.0 34.7 jit_solution(17095167625377766348)
XLA Ops:
  0.6 32.1 %shard_map.103 = (f32[512,128]{1,0:T(8,128)}, f32[8,32,128]{2,1,0:T(8,128)}, f32[768,128]{1,0:T(8,128)}) custom-call(s32[8,8]{1,0:T(8,128)} %bitcast.18, s32[8]{0:T(128)} %bitcast.19, f32[32]{0:T(128)} %fcor_in.1, f32[768,128]{1,0:T(8,128)} %bitcast.10, f32[512,128]{1,0:T(8,128)} %bitcast.12, s32[128,128]{1,0:T(8,128)} %bitcast.15, s32[128,128]{1,0:T(8,128)} %bitcast.16, ...), custom_call_target="tpu_custom_call" | custom-call | flops 30000001024 | bytes 2000000 | tf_op jit(solution)/shard_map/pallas_call | solution.py:364
  32.8 1.9 %shard_map.104 = (f32[512,128]{1,0:T(8,128)}, f32[8,32,128]{2,1,0:T(8,128)}, f32[768,128]{1,0:T(8,128)}) custom-call(f32[512,128]{1,0:T(8,128)} %get-tuple-element.9.refs_0_, f32[8,32,128]{2,1,0:T(8,128)} %get-tuple-element.10.refs_1_, f32[768,128]{1,0:T(8,128)} %get-tuple-element.11.refs_2_), custom_call_target="tpu_custom_call" | custom-call | tf_op jit(solution)/shard_map/pallas_call | solution.py:421

commit v11 on v9

--- a/solution.py
+++ b/solution.py
@@ -324,7 +324,7 @@
     ]
     for each in edges:
         each.start()
-    last((0, 1), 0, STEPS, 4)
+    last((0, 1), 0, STEPS, 8)
     tend[ROWS : 2 * ROWS, :] = -level_diff(deposit(1))
     half = pl.ds(ROWS, ROWS)
     stores.append(pltpu.make_async_copy(tend.at[half], tendency.at[half], store_sem.at[1]))

time: 33.9 us -> 33.9 us (level)
  no operation moved by 1% of the time
where the time goes in v11:
time: 33.9 us; the launch traced here: 33.8 us
  Pallas kernels  33.2 us (98%)
  between operations  0.64 us (2%)
    pallas_call x1, Pallas kernels, on_device(): pl.pallas_call(kernel, out_shape=(jax.ShapeDtypeStruct((NB * 4, 128), F32...  31.2 us
    pallas_call x1, Pallas kernels, on_device(): pl.pallas_call(deliver, out_shape=tuple((jax.ShapeDtypeStruct(each.shape,...  1.94 us

profile of v11, /device:TPU:1, one launch (start us, length us, event | category | flops | bytes accessed | tf_op | source)
XLA Modules:
  0.0 33.8 jit_solution(6711134146923872645)
XLA Ops:
  0.6 31.2 %shard_map.103 = (f32[512,128]{1,0:T(8,128)}, f32[8,32,128]{2,1,0:T(8,128)}, f32[768,128]{1,0:T(8,128)}) custom-call(s32[8,8]{1,0:T(8,128)} %bitcast.18, s32[8]{0:T(128)} %bitcast.19, f32[32]{0:T(128)} %fcor_in.1, f32[768,128]{1,0:T(8,128)} %bitcast.10, f32[512,128]{1,0:T(8,128)} %bitcast.12, s32[128,128]{1,0:T(8,128)} %bitcast.15, s32[128,128]{1,0:T(8,128)} %bitcast.16, ...), custom_call_target="tpu_custom_call" | custom-call | flops 30000001024 | bytes 2000000 | tf_op jit(solution)/shard_map/pallas_call | solution.py:362
  31.9 1.9 %shard_map.104 = (f32[512,128]{1,0:T(8,128)}, f32[8,32,128]{2,1,0:T(8,128)}, f32[768,128]{1,0:T(8,128)}) custom-call(f32[512,128]{1,0:T(8,128)} %get-tuple-element.9.refs_0_, f32[8,32,128]{2,1,0:T(8,128)} %get-tuple-element.10.refs_1_, f32[768,128]{1,0:T(8,128)} %get-tuple-element.11.refs_2_), custom_call_target="tpu_custom_call" | custom-call | tf_op jit(solution)/shard_map/pallas_call | solution.py:419
